TPU v7x, 32 devices: a whole 2x2x4 slice. The times are simulated.
32 devices in a mesh: dp: 8 (over z, y), tensor: 4 (over x, core).
Axes of the slice: x: 2, y: 2, z: 4, core: 2. Of those that a mesh axis runs over, the one named last changes fastest.
Arguments:
- inputs: bfloat16 [4096, 1024], P('dp'), may hold values from -6 to 6
- teacher: bfloat16 [4096, 1024], P('dp'), may hold values from -6 to 6
- lengths: int32 [8], P('dp'), may hold values from 128 to 512, as said below
- expert_ids: int32 [4096, 2], P('dp'), may hold values from 0 to 15, as said below
- route_slots: int32 [4096, 2], P('dp'), may hold values from 0 to 80, as said below
- gain_attn: float32 [1024], replicated, may hold values from 0.5 to 1.5
- w_qkv: bfloat16 [3, 1024, 1024], P(None, None, 'tensor'), may hold values from -0.09375 to 0.09375
- w_out: bfloat16 [1024, 1024], P('tensor'), may hold values from -0.5 to 0.5
- rel_table: float32 [32, 16], P(None, 'tensor'), may hold values from -4 to 4
- gain_moe: float32 [1024], replicated, may hold values from 0.5 to 1.5
- w_router: bfloat16 [1024, 16], replicated, may hold values from -0.09375 to 0.09375
- w_gate_up: bfloat16 [16, 2, 1024, 2816], P('dp', None, None, 'tensor'), may hold values from -0.1875 to 0.1875
- w_down: bfloat16 [16, 2816, 1024], P('dp', 'tensor'), may hold values from -0.21875 to 0.21875
Outputs:
- block_out: float32 [4096, 1024], P('dp', 'tensor')
- loss: float32 [], replicated
- input_grad: float32 [4096, 1024], P('dp', 'tensor')
- gain_attn_grad: float32 [1024], replicated
- qkv_grad: float32 [3, 1024, 1024], P(None, None, 'tensor')
- out_proj_grad: float32 [1024, 1024], P('tensor')
- table_grad: float32 [32, 16], P(None, 'tensor')
- gain_moe_grad: float32 [1024], replicated
- router_grad: float32 [1024, 16], replicated
- gate_up_grad: float32 [16, 2, 1024, 2816], P('dp', None, None, 'tensor')
- down_grad: float32 [16, 2816, 1024], P('dp', 'tensor')
Inputs may be any that keep to these rules, and one draw needn't show every extreme that they name: The first sequence has 128 valid tokens and the last 512; between them lengths grow with the sequence's index, each shortened at random. `expert_ids`: a token's two experts differ. `route_slots`: within the tokens of one index of dp, first routes take slots in token order before second routes, and each expert's slots are 0, 1, 2 and so on; 80 marks a route that is dropped or whose token is padding; some expert receives 80 routes from every index of dp.
All inputs are finite; a program needn't handle non-finite values.
Results may differ from a plain program's by a relative error of at most 0.018.
The roundings to bfloat16 on the way count: a program that leaves them out, or rounds other values in their place, can miss the bound.
Values may be sent and summed in bfloat16 or wider, within the bound.
A program may use at most 320 MiB of HBM per device.

v0:
```python
import jax
import jax.numpy as jnp
from jax import lax
from jax.sharding import PartitionSpec as P

BUCKETS = 32
SEQ_LEN = 512


EPSILON = 1e-06
FAR_STEPS = (12, 16, 23, 32, 46, 64, 91)
MASKED = -1000000000.0


def offset_bucket(offset):
    direction = jnp.where(offset > 0, 16, 0).astype(jnp.int32)
    distance = jnp.abs(offset)
    farther = jnp.full(offset.shape, 8, jnp.int32)
    for threshold in FAR_STEPS:
        farther = farther + (distance >= threshold).astype(jnp.int32)
    return direction + jnp.where(distance < 8, distance, farther)


def bucket_onehot(offsets):
    bucket_range = jnp.arange(BUCKETS, dtype=jnp.int32)
    return (offset_bucket(offsets)[:, None] == bucket_range[None, :]).astype(jnp.float32)


def diagonal_sums(score_grad):
    heads_here, query_rows, key_rows = score_grad.shape
    flipped = score_grad[:, ::-1, :]
    padded = jnp.pad(flipped, ((0, 0), (0, 0), (0, query_rows)))
    flat = padded.reshape(heads_here, query_rows * (key_rows + query_rows))
    flat = flat[:, : query_rows * (key_rows + query_rows - 1)]
    skewed = flat.reshape(heads_here, query_rows, key_rows + query_rows - 1)
    return jnp.sum(skewed, axis=1)


def rms_norm(values, gain):
    return values * lax.rsqrt(jnp.mean(values * values, axis=-1, keepdims=True) + EPSILON) * gain


def route_gates(logits, picks):
    expert_probs = jax.nn.softmax(logits, axis=-1)
    chosen = jnp.sum(expert_probs[:, None, :] * picks, axis=-1)
    return chosen / jnp.sum(chosen, axis=-1, keepdims=True)


def gelu_tanh(values):
    return jax.nn.gelu(values, approximate=True)


def body(
    inputs,
    teacher,
    lengths,
    expert_ids,
    route_slots,
    gain_attn,
    w_qkv,
    w_out,
    rel_table,
    gain_moe,
    w_router,
    w_gate_up,
    w_down,
):
    highest = lax.Precision.HIGHEST
    tok_rows, model_width = inputs.shape
    groups = lax.axis_size("dp")
    shards = lax.axis_size("tensor")
    experts = w_router.shape[1]
    local_experts = w_gate_up.shape[0]
    capacity = 10 * tok_rows // (4 * experts)
    slot_count = experts * capacity
    heads_here = rel_table.shape[1]
    head_width = w_qkv.shape[2] // heads_here
    block_rows = min(512, SEQ_LEN)
    blocks_per = SEQ_LEN // block_rows
    seq_here = tok_rows // SEQ_LEN
    part_width = model_width // shards
    column_start = lax.axis_index("tensor") * part_width
    all_offsets = jnp.arange(2 * SEQ_LEN - 1, dtype=jnp.int32) - (SEQ_LEN - 1)
    offset_bias = jnp.dot(bucket_onehot(all_offsets), rel_table, precision=highest).T
    diag_offsets = jnp.arange(block_rows + SEQ_LEN - 1, dtype=jnp.int32) - (block_rows - 1)
    residual = inputs.astype(jnp.float32)
    normed_one, norm_one_pull = jax.vjp(rms_norm, residual, gain_attn)
    normed_low = normed_one.astype(jnp.bfloat16)
    projected = jnp.einsum(
        "td,jde->jte", normed_low, w_qkv, preferred_element_type=jnp.float32
    ).astype(jnp.bfloat16)
    queries = projected[0].reshape(tok_rows, heads_here, head_width)
    keys_all = projected[1].reshape(tok_rows, heads_here, head_width)
    values_all = projected[2].reshape(tok_rows, heads_here, head_width)
    positions = jnp.arange(SEQ_LEN, dtype=jnp.int32)

    def block_view(block_index):
        seq_index = block_index // blocks_per
        query_start = block_index % blocks_per * block_rows
        key_alive = positions < lax.dynamic_index_in_dim(lengths, seq_index, 0, keepdims=False)
        query_pos = query_start + jnp.arange(block_rows, dtype=jnp.int32)
        lookup = positions[None, :] - query_pos[:, None] + (SEQ_LEN - 1)
        bias = jnp.take(offset_bias, lookup, axis=1)
        scores = (
            jnp.einsum("qhe,khe->hqk", queries, keys_all, preferred_element_type=jnp.float32) + bias
        )
        scores = jnp.where(key_alive[None, None, :], scores, MASKED)
        return (queries, keys_all, values_all, query_start, scores)

    def forward_block(block_index):
        pieces = block_view(block_index)
        maximum = jnp.max(pieces[4], axis=-1, keepdims=True)
        exponent = jnp.exp(pieces[4] - maximum)
        denominator = jnp.sum(exponent, axis=-1, keepdims=True)
        weights = (exponent / denominator).astype(jnp.bfloat16)
        mixture = jnp.einsum("hqk,khe->qhe", weights, pieces[2], preferred_element_type=jnp.float32)
        return (
            mixture.reshape(block_rows, heads_here * head_width),
            (maximum + jnp.log(denominator))[..., 0],
        )

    mixture_blocks, log_totals = lax.map(
        forward_block, jnp.arange(seq_here * blocks_per, dtype=jnp.int32)
    )
    attended = mixture_blocks.reshape(tok_rows, heads_here * head_width).astype(jnp.bfloat16)
    attn_out = lax.psum(jnp.dot(attended, w_out, preferred_element_type=jnp.float32), "tensor")
    after_attn = residual + attn_out
    normed_two, norm_two_pull = jax.vjp(rms_norm, after_attn, gain_moe)
    normed_two_low = normed_two.astype(jnp.bfloat16)
    logits = jnp.dot(normed_two_low, w_router, preferred_element_type=jnp.float32)
    expert_range = jnp.arange(experts, dtype=jnp.int32)
    picks = (expert_ids[:, :, None] == expert_range[None, None, :]).astype(jnp.float32)
    gates, gate_pull = jax.vjp(lambda values: route_gates(values, picks), logits)
    kept_route = route_slots < capacity
    target = jnp.where(kept_route, expert_ids * capacity + route_slots, -1)
    slot_range = jnp.arange(slot_count, dtype=jnp.int32)
    onehot_routes = (target[:, :, None] == slot_range[None, None, :]).astype(jnp.bfloat16)
    dispatched = jnp.einsum(
        "tks,td->sd", onehot_routes, normed_two_low, preferred_element_type=jnp.float32
    ).astype(jnp.bfloat16)
    dispatched = dispatched.reshape(groups, local_experts, capacity, model_width)

    def to_experts(slot_rows):
        arrived = lax.all_to_all(slot_rows, "dp", split_axis=0, concat_axis=0, tiled=True)
        return arrived

    expert_rows = to_experts(dispatched)
    gate_up = jnp.einsum(
        "nxcd,xjdf->jnxcf", expert_rows, w_gate_up, preferred_element_type=jnp.float32
    )
    activated, gelu_pull = jax.vjp(gelu_tanh, gate_up[0])
    hidden_low = (activated * gate_up[1]).astype(jnp.bfloat16)
    partial_out = jnp.einsum(
        "nxcf,xfd->nxcd", hidden_low, w_down, preferred_element_type=jnp.float32
    ).astype(jnp.bfloat16)
    returned = lax.all_to_all(partial_out, "dp", split_axis=0, concat_axis=0, tiled=True).reshape(
        slot_count, model_width
    )
    routed = jnp.einsum("tks,sd->tkd", onehot_routes, returned, preferred_element_type=jnp.float32)
    moe_part = gates[:, 0, None] * routed[:, 0] + gates[:, 1, None] * routed[:, 1]
    row_index = jnp.arange(tok_rows, dtype=jnp.int32)
    seq_of_row = row_index // SEQ_LEN
    row_len = jnp.sum(
        jnp.where(
            seq_of_row[:, None] == jnp.arange(seq_here, dtype=jnp.int32)[None, :],
            lengths[None, :],
            0,
        ),
        axis=1,
    )
    row_alive = (row_index % SEQ_LEN < row_len).astype(jnp.float32)[:, None]
    valid_total = lax.psum(jnp.sum(lengths).astype(jnp.float32), "dp")
    scale = groups * tok_rows / valid_total
    moe_out = lax.psum(moe_part, "tensor")
    block_out = after_attn + moe_out
    deviation = (block_out - teacher.astype(jnp.float32)) * row_alive
    out_share = lax.dynamic_slice_in_dim(block_out, column_start, part_width, 1)
    deviation_share = lax.dynamic_slice_in_dim(deviation, column_start, part_width, 1)
    out_grad = deviation * scale
    squared = lax.psum(jnp.sum(deviation_share * deviation_share), ("dp", "tensor"))
    loss = squared / (2.0 * valid_total * model_width)
    gated_grad = (gates[:, :, None] * out_grad[:, None, :]).astype(jnp.bfloat16)
    slot_grad = jnp.einsum(
        "tks,tkd->sd", onehot_routes, gated_grad, preferred_element_type=jnp.float32
    ).astype(jnp.bfloat16)
    slot_grad = slot_grad.reshape(groups, local_experts, capacity, model_width)
    gate_grad_part = jnp.sum(routed * out_grad[:, None, :], axis=-1)
    expert_grad = to_experts(slot_grad)
    down_grad = jnp.einsum(
        "nxcf,nxcd->xfd", hidden_low, expert_grad, preferred_element_type=jnp.float32
    )
    hidden_grad = jnp.einsum(
        "nxcd,xfd->nxcf", expert_grad, w_down, preferred_element_type=jnp.float32
    )
    gate_side = gelu_pull(hidden_grad * gate_up[1])[0]
    up_side = hidden_grad * activated
    pre_grads = jnp.stack([gate_side, up_side], axis=0).astype(jnp.bfloat16)
    gate_up_grad = jnp.einsum(
        "nxcd,jnxcf->xjdf", expert_rows, pre_grads, preferred_element_type=jnp.float32
    )
    rows_grad = jnp.einsum(
        "jnxcf,xjdf->nxcd", pre_grads, w_gate_up, preferred_element_type=jnp.float32
    )
    onehot_wide = onehot_routes.astype(jnp.float32)
    back_grad = (
        lax.all_to_all(
            rows_grad.astype(jnp.bfloat16), "dp", split_axis=0, concat_axis=0, tiled=True
        )
        .astype(rows_grad.dtype)
        .reshape(slot_count, model_width)
    )
    normed_grad_part = jnp.einsum("tks,sd->td", onehot_wide, back_grad, precision=highest)
    normed_grad_moe, gate_grad = lax.psum((normed_grad_part, gate_grad_part), "tensor")
    logit_grad = gate_pull(gate_grad)[0].astype(jnp.bfloat16)
    router_grad = jnp.dot(normed_two_low.T, logit_grad, preferred_element_type=jnp.float32)
    normed_two_grad = normed_grad_moe + jnp.dot(
        logit_grad, w_router.T, preferred_element_type=jnp.float32
    )
    after_grad_norm, gain_moe_grad = norm_two_pull(normed_two_grad)
    after_grad = out_grad + after_grad_norm
    branch_grad = after_grad.astype(jnp.bfloat16)
    out_proj_grad = jnp.dot(attended.T, branch_grad, preferred_element_type=jnp.float32)
    attended_grad = jnp.dot(branch_grad, w_out.T, preferred_element_type=jnp.float32).astype(
        jnp.bfloat16
    )
    attended_grad = attended_grad.reshape(tok_rows, heads_here, head_width)

    def sequence_back(table_carry, seq_index):

        def block_back(carry, block_pos):
            key_grad, value_grad, table_acc = carry
            block_index = seq_index * blocks_per + block_pos
            pieces = block_view(block_index)
            log_total = lax.dynamic_index_in_dim(log_totals, block_index, 0, keepdims=False)
            probs = jnp.exp(pieces[4] - log_total[..., None])
            value_grad = value_grad + jnp.einsum(
                "hqk,qhe->khe",
                probs.astype(jnp.bfloat16),
                attended_grad,
                preferred_element_type=jnp.float32,
            )
            prob_grad = jnp.einsum(
                "qhe,khe->hqk", attended_grad, pieces[2], preferred_element_type=jnp.float32
            )
            score_grad = probs * (prob_grad - jnp.sum(probs * prob_grad, axis=-1, keepdims=True))
            per_offset = diagonal_sums(score_grad)
            table_acc = table_acc + jnp.dot(
                bucket_onehot(diag_offsets - pieces[3]).T, per_offset.T, precision=highest
            )
            score_low = score_grad.astype(jnp.bfloat16)
            query_grad = jnp.einsum(
                "hqk,khe->qhe", score_low, pieces[1], preferred_element_type=jnp.float32
            )
            key_grad = key_grad + jnp.einsum(
                "hqk,qhe->khe", score_low, pieces[0], preferred_element_type=jnp.float32
            )
            return ((key_grad, value_grad, table_acc), query_grad)

        zero_rows = jnp.zeros((SEQ_LEN, heads_here, head_width), jnp.float32)
        final_carry, query_grads = lax.scan(
            block_back, (zero_rows, zero_rows, table_carry), jnp.arange(blocks_per, dtype=jnp.int32)
        )
        width_here = heads_here * head_width
        return (
            final_carry[2],
            (
                query_grads.reshape(SEQ_LEN, width_here),
                final_carry[0].reshape(SEQ_LEN, width_here),
                final_carry[1].reshape(SEQ_LEN, width_here),
            ),
        )

    table_grad, seq_grads = lax.scan(
        sequence_back,
        jnp.zeros(rel_table.shape, jnp.float32),
        jnp.arange(seq_here, dtype=jnp.int32),
    )
    query_all = seq_grads[0].reshape(tok_rows, -1)
    key_all = seq_grads[1].reshape(tok_rows, -1)
    value_all = seq_grads[2].reshape(tok_rows, -1)
    projected_grad = jnp.stack([query_all, key_all, value_all], axis=0).astype(jnp.bfloat16)
    qkv_grad = jnp.einsum(
        "td,jte->jde", normed_low, projected_grad, preferred_element_type=jnp.float32
    )
    normed_one_part = jnp.einsum(
        "jte,jde->td", projected_grad, w_qkv, preferred_element_type=jnp.float32
    )
    normed_one_grad = lax.psum(normed_one_part.astype(jnp.bfloat16), "tensor").astype(jnp.float32)
    input_grad_norm, gain_attn_grad = norm_one_pull(normed_one_grad)
    input_grad = after_grad + input_grad_norm
    dense = (
        lax.psum(gain_attn_grad.astype(jnp.bfloat16), "dp").astype(jnp.float32),
        lax.psum(gain_moe_grad.astype(jnp.bfloat16), "dp").astype(jnp.float32),
        lax.psum(router_grad.astype(jnp.bfloat16), "dp").astype(jnp.float32),
        lax.psum(qkv_grad.astype(jnp.bfloat16), "dp").astype(jnp.float32),
        lax.psum(out_proj_grad.astype(jnp.bfloat16), "dp").astype(jnp.float32),
        lax.psum(table_grad.astype(jnp.bfloat16), "dp").astype(jnp.float32),
    )
    input_share = lax.dynamic_slice_in_dim(input_grad, column_start, part_width, 1)
    return (
        out_share,
        loss,
        input_share,
        dense[0],
        dense[3],
        dense[4],
        dense[5],
        dense[1],
        dense[2],
        gate_up_grad,
        down_grad,
    )


def solution(mesh):
    placed = (
        P("dp", None),
        P("dp", None),
        P("dp"),
        P("dp", None),
        P("dp", None),
        P(),
        P(None, None, "tensor"),
        P("tensor", None),
        P(None, "tensor"),
        P(),
        P(),
        P("dp", None, None, "tensor"),
        P("dp", "tensor", None),
    )
    return jax.shard_map(
        body,
        mesh=mesh,
        in_specs=placed,
        out_specs=(
            P("dp", "tensor"),
            P(),
            P("dp", "tensor"),
            P(),
            P(None, None, "tensor"),
            P("tensor", None),
            P(None, "tensor"),
            P(),
            P(),
            P("dp", None, None, "tensor"),
            P("dp", "tensor", None),
        ),
        check_vma=False,
    )
```

profile of v0, /device:TPU:0, one launch (start us, length us, event | category | flops | bytes accessed | tf_op | source)
XLA Modules:
  0.0 1727.8 jit_solution(4809328644363096620)
XLA Ops:
  7.3 1.1 fusion.58
  9.2 1.5 multiply_reduce_fusion.6
  11.3 2.9 fusion.50
  16.4 1.5 copy.149
  17.9 1.1 broadcast_clamp_fusion
  19.0 949.1 %gather_fusion = f32[262144,4]{1,0:T(8,128)} fusion(f32[4,1023]{0,1:T(8,128)S(1)} %copy.100, s32[262144]{0:T(1024)} %broadcast_clamp_fusion), kind=kCustom, calls=%fused_computation.clone | custom fusion | bytes 9437184 | tf_op jit(solution)/shard_map/while/body/eval_jaxpr/jit(_take)/gather | solution.py:103
  968.1 71.7 %copy.102 = f32[512,512,4]{0,1,2:T(8,128)} copy(f32[512,512,4]{2,1,0:T(8,128)} %bitcast.7) | data formatting | bytes 8388608 | tf_op jit(solution)/shard_map/while/body/eval_jaxpr/jit(_take)/gather | solution.py:103
  1039.9 2.0 copy.99
  1041.9 3.6 fusion.95
  1048.1 1.8 fusion.101
  1050.0 2.7 convert_reduce_fusion
  1052.7 51.5 %all-reduce.9.cloned.1.call-done = f32[512,1024]{1,0:T(8,128)} async-done(((f32[512,1024]{1,0:T(8,128)}), f32[512,1024]{1,0:T(8,128)}) %all-reduce.9.cloned.1.call-update) | async-done | bytes 2097168 | tf_op jit(solution)/shard_map/psum | solution.py:126
  1104.2 2.2 multiply_reduce_fusion.5
  1106.4 1.4 copy-done.5
  1108.9 1.5 fusion.103
  1110.4 65.2 %all_to_all.20 = bf16[8,2,80,1024]{3,2,1,0:T(8,128)(2,1)S(1)} all-to-all(bf16[8,2,80,1024]{3,2,1,0:T(8,128)(2,1)S(1)} %bitcast.193), channel_id=1, replica_groups=mesh['dp'=8,'tensor'=4] {'dp'}, dimensions={0} | all-to-all | bytes 5242880 | tf_op jit(solution)/shard_map/all_to_all | solution.py:144
  1175.6 4.3 fusion.20
  1179.9 1.4 multiply_convert_fusion.1
  1181.3 1.8 copy-done.14
  1183.1 2.3 convert_bitcast_fusion
  1185.4 1.9 copy.106
  1187.3 4.5 all-to-all-start.1
  1191.9 1.6 fusion.96
  1193.6 56.8 %all-to-all-done.1 = bf16[8,2,80,1024]{3,2,1,0:T(8,128)(2,1)} async-done(((bf16[8,2,80,1024]{3,2,1,0:T(8,128)(2,1)}), bf16[8,2,80,1024]{3,2,1,0:T(8,128)(2,1)}, u32[]{:S(2)}, u32[]{:S(2)}) %all-to-all-start.1) | async-done | bytes 2621472 | tf_op jit(solution)/shard_map/all_to_all | solution.py:156
  1250.4 4.8 fusion.5
  1255.3 2.0 copy-done.12
  1257.3 1.7 fusion.39
  1259.0 20.1 %psum.94 = f32[]{:T(128)} all-reduce(f32[]{:T(128)S(6)} %convert_element_type.284), channel_id=1, replica_groups=mesh['dp'=8,'tensor'=4] {'dp'}, use_global_device_ids=true, to_apply=%region_13.15 | all-reduce | flops 1 | bytes 8 | tf_op jit(solution)/shard_map/psum | solution.py:172
  1279.8 29.0 %all-reduce.11.cloned.1.call-done = f32[512,1024]{1,0:T(8,128)} async-done(((f32[512,1024]{1,0:T(8,128)}), f32[512,1024]{1,0:T(8,128)}) %all-reduce.11.cloned.1.call-update) | async-done | bytes 2097168 | tf_op jit(solution)/shard_map/psum | solution.py:174
  1308.8 5.1 broadcast_multiply_fusion
  1313.9 3.3 bitcast_convert_fusion.1
  1317.3 65.0 %all_to_all.21 = bf16[8,2,80,1024]{3,2,1,0:T(8,128)(2,1)S(1)} all-to-all(bf16[8,2,80,1024]{3,2,1,0:T(8,128)(2,1)S(1)} %bitcast.192), channel_id=1, replica_groups=mesh['dp'=8,'tensor'=4] {'dp'}, dimensions={0} | all-to-all | bytes 5242880 | tf_op jit(solution)/shard_map/all_to_all | solution.py:144
  1382.3 5.0 fusion.48
  1387.3 4.4 fusion.2
  1392.2 1.8 copy.110
  1394.0 4.4 all-to-all-start.3
  1398.5 3.0 convert_element_type.260
  1402.1 1.8 multiply_reduce_fusion.7
  1403.9 73.2 %psum.93 = f32[]{:T(128)} all-reduce(f32[]{:T(128)} %multiply_reduce_fusion.7), channel_id=1, replica_groups=mesh['dp'=8,'tensor'=4] {'dp','tensor'}, use_global_device_ids=true, to_apply=%region_12.14 | all-reduce | flops 1 | bytes 8 | tf_op jit(solution)/shard_map/psum | solution.py:180
  1477.1 2.7 multiply_reduce_fusion.1
  1479.8 6.2 psum.96
  1486.1 8.1 fusion.102
  1495.1 1.9 constant_dynamic-slice_fusion
  1497.0 1.5 convolution_convert_fusion.7
  1498.5 47.0 %all-reduce.13.cloned.1.call-done = f32[512,1024]{1,0:T(8,128)} async-done(((f32[512,1024]{1,0:T(8,128)}), f32[512,1024]{1,0:T(8,128)}) %all-reduce.13.cloned.1.call-update) | async-done | bytes 2097168 | tf_op jit(solution)/shard_map/psum | solution.py:213
  1545.5 2.5 multiply_reduce_fusion.2
  1549.6 1.6 copy-done.3
  1552.1 1.1 subtract_multiply_fusion
  1556.4 3.5 bitcast_convert_fusion.2
  1560.3 1.2 convolution_convert_fusion.3
  1561.5 3.5 fusion.49
  1565.1 12.2 convolution_bitcast_fusion
  1577.3 5.0 convolution_bitcast_fusion.1
  1582.4 34.8 %rev.5 = f32[4,512,512]{1,2,0:T(8,128)} reverse(f32[4,512,512]{1,2,0:T(8,128)} %copy-done.4), dimensions={1} | reverse | bytes 8388608 | tf_op jit(solution)/shard_map/while/body/eval_jaxpr/while/body/eval_jaxpr/rev | solution.py:31
  1617.2 5.3 copy.148
  1622.5 6.7 pad_bitcast_fusion
  1629.1 12.0 copy.150
  1641.2 7.3 slice.54
  1648.4 15.7 reshape.275
  1664.1 4.0 reduce_sum.198
  1668.6 3.8 fusion.34
  1672.3 38.7 %all-reduce.1 = (bf16[1024]{0:T(1024)(128)(2,1)S(1)}, bf16[32,4]{0,1:T(4,128)(2,1)S(1)}, bf16[1024]{0:T(1024)(128)(2,1)S(1)}, bf16[1024,16]{0,1:T(8,128)(2,1)S(1)}) all-reduce(bf16[1024]{0:T(1024)(128)(2,1)S(1)} %get-tuple-element.187, bf16[32,4]{0,1:T(4,128)(2,1)S(1)} %convolution_convert_fusion.8, ...), channel_id=1, replica_groups=mesh['dp'=8,'tensor'=4] {'dp'}, use_global_device_ids=true, to_apply=%region_25.27 | all-reduce | flops 18560 | bytes 74240 | tf_op jit(solution)/shard_map/psum | solution.py:292
  1713.4 2.2 fusion.64
  1715.7 3.2 copy.122
  (158 shorter events, 17.5 us)
Async XLA Ops:
  7.2 1175.9 %copy-start = (bf16[2,704,1024]{2,1,0:T(8,128)(2,1)S(1)}, bf16[2,704,1024]{2,1,0:T(8,128)(2,1)}, u32[]{:S(2)}) copy-start(bf16[2,704,1024]{2,1,0:T(8,128)(2,1)} %param.27) | copy-start | bytes 8650756
  7.2 1097.0 %all-reduce.9.cloned.1.call-start = ((), (), s32[]{:S(2)}) async-start(), calls=%async_computation.4 | async-start | bytes 4194304 | tf_op jit(solution)/shard_map/psum | solution.py:126
  7.3 8.4 copy-start.38
  10.7 0.6 copy-start.35
  11.3 3.8 copy-start.33
  11.3 4.4 copy-start.41
  968.1 73.7 %copy-start.19 = (bf16[1,512,256]{1,2,0:T(8,128)(2,1)S(1)}, bf16[1,512,256]{1,2,0:T(8,128)(2,1)}, u32[]{:S(2)}) copy-start(bf16[1,512,256]{1,2,0:T(8,128)(2,1)} %get-tuple-element.206) | copy-start | bytes 786436
  968.1 73.7 %copy-start.20 = (bf16[1,512,256]{1,2,0:T(8,128)(2,1)S(1)}, bf16[1,512,256]{1,2,0:T(8,128)(2,1)}, u32[]{:S(2)}) copy-start(bf16[1,512,256]{1,2,0:T(8,128)(2,1)} %get-tuple-element.205) | copy-start | bytes 786436
  1045.4 2.0 copy-start.2
  1045.4 1.1 copy-start.25
  1046.6 1.6 copy-start.21
  1047.4 0.7 copy-start.27
  1047.4 2.5 copy-start.32
  1047.5 2.5 copy-start.37
  1052.7 55.1 %copy-start.31 = (f32[1024]{0:T(1024)S(1)}, f32[1024]{0:T(1024)}, u32[]{:S(2)}) copy-start(f32[1024]{0:T(1024)} %param.24) | copy-start | bytes 12292
  1106.4 1.4 copy-start.5
  1106.4 2.5 copy-start.18
  1107.8 67.8 %slice-start.2 = ((s8[5767168]{0:T(1024)(128)(4,1)}), s8[4194304]{0:T(1024)(128)(4,1)S(1)}, s32[]{:S(2)}) async-start(s8[5767168]{0:T(1024)(128)(4,1)} %bitcast.209), calls=%async_computation.11 | async-start | bytes 8388608
  1108.9 1.5 copy-start.13
  1108.9 66.7 %slice-start.3 = ((s8[5767168]{0:T(1024)(128)(4,1)}), s8[1572864]{0:T(1024)(128)(4,1)S(1)}, s32[]{:S(2)}) async-start(s8[5767168]{0:T(1024)(128)(4,1)} %bitcast.209), calls=%async_computation.12 | async-start | bytes 3145728
  1175.6 4.3 copy-start.15
  1179.9 3.2 copy-start.14
  1183.1 2.3 copy-start.23
  1187.3 4.6 copy-start.30
  1187.3 63.2 %all-to-all-start.1 = ((bf16[8,2,80,1024]{3,2,1,0:T(8,128)(2,1)}), bf16[8,2,80,1024]{3,2,1,0:T(8,128)(2,1)}, u32[]{:S(2)}, u32[]{:S(2)}) async-start(bf16[8,2,80,1024]{3,2,1,0:T(8,128)(2,1)} %copy.106), calls=%async_computation.1 | async-start | bytes 5242880 | tf_op jit(solution)/shard_map/all_to_all | solution.py:156
  1191.8 117.0 %all-reduce.11.cloned.1.call-start = ((), (), s32[]{:S(2)}) async-start(), calls=%async_computation.5 | async-start | bytes 4194304 | tf_op jit(solution)/shard_map/psum | solution.py:174
  1255.3 2.0 copy-start.12
  1308.8 73.4 %slice-start = ((s8[7864320]{0:T(1024)(128)(4,1)}), s8[4194304]{0:T(1024)(128)(4,1)S(1)}, s32[]{:S(2)}) async-start(s8[7864320]{0:T(1024)(128)(4,1)} %bitcast.189), calls=%async_computation.9 | async-start | bytes 8388608
  1313.9 3.3 copy-start.9
  1313.9 68.3 %slice-start.1 = ((s8[7864320]{0:T(1024)(128)(4,1)}), s8[3670016]{0:T(1024)(128)(4,1)S(1)}, s32[]{:S(2)}) async-start(s8[7864320]{0:T(1024)(128)(4,1)} %bitcast.189), calls=%async_computation.10 | async-start | bytes 7340032
  1317.3 70.0 %slice-start.4 = ((s8[5767168]{0:T(1024)(128)(4,1)}), s8[4194304]{0:T(1024)(128)(4,1)S(1)}, s32[]{:S(2)}) async-start(s8[5767168]{0:T(1024)(128)(4,1)} %bitcast.211), calls=%async_computation.13 | async-start | bytes 8388608
  1382.3 5.0 copy-start.16
  1382.3 5.0 slice-start.5
  1387.3 4.5 copy-start.42
  1387.3 4.5 copy-start.43
  1394.0 92.1 %all-to-all-start.3 = ((bf16[8,2,80,1024]{3,2,1,0:T(8,128)(2,1)}), bf16[8,2,80,1024]{3,2,1,0:T(8,128)(2,1)}, u32[]{:S(2)}, u32[]{:S(2)}) async-start(bf16[8,2,80,1024]{3,2,1,0:T(8,128)(2,1)} %copy.110), calls=%async_computation.3 | async-start | bytes 5242880 | tf_op jit(solution)/shard_map/all_to_all | solution.py:206
  1398.4 78.7 %copy-start.10 = (f32[512,1024]{1,0:T(8,128)S(1)}, f32[512,1024]{1,0:T(8,128)}, u32[]{:S(2)}) copy-start(f32[512,1024]{1,0:T(8,128)} %copy-done.9) | copy-start | bytes 6291460
  1398.4 147.1 %all-reduce.13.cloned.1.call-start = ((), (), s32[]{:S(2)}) async-start(), calls=%async_computation.6 | async-start | bytes 4194304 | tf_op jit(solution)/shard_map/psum | solution.py:213
  1494.2 51.3 %copy-start.6 = (f32[512,1024]{1,0:T(8,128)S(1)}, f32[512,1024]{1,0:T(8,128)}, u32[]{:S(2)}) copy-start(f32[512,1024]{1,0:T(8,128)} %copy-done.5) | copy-start | bytes 6291460
  1494.2 174.3 %all-reduce.15.cloned.1.call-start = ((), (), s32[]{:S(2)}) async-start(), calls=%async_computation.7 | async-start | bytes 2097152 | tf_op jit(solution)/shard_map/psum | solution.py:288
  1545.5 2.5 copy-start.11
  1548.0 1.0 copy-start.22
  1548.0 3.1 copy-start.3
  1549.1 3.0 copy-start.7
  1549.1 2.1 copy-start.26
  1553.2 1.9 copy-start.4
  1556.4 3.9 copy-start.8
  1556.4 3.9 copy-start.28
  1559.9 1.6 copy-start.34
  1559.9 1.6 copy-start.40
  1560.0 155.7 %all-reduce.17.cloned.1.call-start = ((), (), s32[]{:S(2)}) async-start(), calls=%async_computation.8 | async-start | bytes 4194304 | tf_op jit(solution)/shard_map/psum | solution.py:295
  1565.1 12.3 copy-start.17
  1565.1 12.2 copy-start.24
  1664.1 4.0 copy-start.39
  1668.1 45.3 %copy-start.36 = (f32[512]{0:T(512)S(1)}, f32[512]{0:T(512)}, u32[]{:S(2)}) copy-start(f32[512]{0:T(512)} %copy-done.35) | copy-start | bytes 6148
  1715.6 3.2 copy-start.29
  1715.7 4.3 copy-start.1
Sparse Core Ops, SparseCore 0:
  1050.1 54.0 all-reduce.8
  1259.1 49.6 all-reduce.10
  1494.3 51.0 all-reduce.12
  1560.1 36.4 all-reduce.14
  1600.1 104.0 all-reduce.16
where the time goes:
time: 1760 us; the launch traced here: 1730 us
  local copies, waits for them, and re-layouts  1130 us (64%)
  blocking collectives  268 us (15%)
  waiting for transfers between devices  184 us (10%)
  matrix products  78.2 us (4%)
  other arithmetic  41.2 us (2%)
  between operations  18.6 us (1%)
    gather x2, local copies, waits for them, and re-layouts, block_view(): bias = jnp.take(offset_bias, lookup, axis=1)  1020 us
    all_to_all x2, blocking collectives, to_experts(): lax.all_to_all(slot_rows, 'dp', split_axis=0, concat_axis=0, tiled=True)  130 us
    psum x1, blocking collectives, body(): lax.psum(jnp.sum(deviation_share * deviation_share), ('dp', 'tensor'))  73.2 us
    all_to_all x1, waiting for transfers between devices, body(): lax.all_to_all(partial_out, 'dp', split_axis=0, concat_axis=0, tiled=True)  56.8 us
    psum x1, waiting for transfers between devices, body(): lax.psum(jnp.dot(attended, w_out, preferred_element_type=jnp.float32), 't...  51.5 us
    psum x1, waiting for transfers between devices, body(): lax.psum((normed_grad_part, gate_grad_part), 'tensor')  47 us
    unnamed x105, local copies, waits for them, and re-layouts  39.5 us
    psum x1, blocking collectives, body(): lax.psum(gain_attn_grad.astype(jnp.bfloat16), 'dp').astype(jnp.float32)  38.7 us
  transfers between devices with their start and end apart: 7, of which 4 were waited for; matrix products, arithmetic and copies ran while one was open for 8% of the time, Pallas kernels for 0%

commit v1 on v0

v1 whole, which is shorter than its diff:
```python
import functools
import math

import jax
import jax.numpy as jnp
from jax import lax
from jax.experimental import pallas as pl
from jax.experimental.pallas import tpu as pltpu
from jax.sharding import PartitionSpec as P

BUCKETS = 32
SEQ_LEN = 512
TILE = 128
SPAN = 2 * SEQ_LEN

EPSILON = 1e-06
FAR_STEPS = (12, 16, 23, 32, 46, 64, 91)
MASKED = -1000000000.0
F32 = jnp.float32
BF16 = jnp.bfloat16


def offset_bucket(offset):
    direction = jnp.where(offset > 0, 16, 0).astype(jnp.int32)
    distance = jnp.abs(offset)
    farther = jnp.full(offset.shape, 8, jnp.int32)
    for threshold in FAR_STEPS:
        farther = farther + (distance >= threshold).astype(jnp.int32)
    return direction + jnp.where(distance < 8, distance, farther)


def bucket_onehot(offsets):
    bucket_range = jnp.arange(BUCKETS, dtype=jnp.int32)
    return (offset_bucket(offsets)[:, None] == bucket_range[None, :]).astype(F32)


def route_gates(logits, picks):
    expert_probs = jax.nn.softmax(logits, axis=-1)
    chosen = jnp.sum(expert_probs[:, None, :] * picks, axis=-1)
    return chosen / jnp.sum(chosen, axis=-1, keepdims=True)


def dot(a, b, dims=((1,), (0,))):
    return lax.dot_general(a, b, (dims, ((), ())), preferred_element_type=F32)


def attention_forward(heads, width, len_ref, bias_ref, proj_ref, attended_ref, probs_ref):
    length = len_ref[0]
    alive = lax.broadcasted_iota(jnp.int32, (TILE, SEQ_LEN), 1) < length
    for h in range(heads):
        cols = slice(h * width, (h + 1) * width)
        keys = proj_ref[1, :, cols]
        values = proj_ref[2, :, cols]
        skew = pltpu.roll(
            jnp.broadcast_to(bias_ref[h : h + 1, :], (TILE, SPAN)), 0, 1, stride=1, stride_axis=0
        )
        for j in range(SEQ_LEN // TILE):
            rows = slice(j * TILE, (j + 1) * TILE)
            start = SEQ_LEN - j * TILE
            scores = dot(proj_ref[0, rows, cols], keys, ((1,), (1,)))
            scores = jnp.where(alive, scores + skew[:, start : start + SEQ_LEN], MASKED)
            exponent = jnp.exp(scores - jnp.max(scores, axis=1, keepdims=True))
            probs = exponent * (1.0 / jnp.sum(exponent, axis=1, keepdims=True))
            probs_ref[h, rows, :] = probs
            attended_ref[rows, cols] = dot(probs.astype(BF16), values).astype(BF16)


def attention_backward(heads, width, proj_ref, probs_ref, grad_ref, out_ref, diag_ref, acc, key_acc, value_acc):
    for h in range(heads):
        cols = slice(h * width, (h + 1) * width)
        keys = proj_ref[1, :, cols]
        values = proj_ref[2, :, cols]
        acc[...] = jnp.zeros_like(acc)
        for j in range(SEQ_LEN // TILE):
            rows = slice(j * TILE, (j + 1) * TILE)
            start = SEQ_LEN - j * TILE
            probs = probs_ref[h, rows, :]
            grad = grad_ref[rows, cols]
            prob_grad = dot(grad, values, ((1,), (1,)))
            score_grad = probs * (prob_grad - jnp.sum(probs * prob_grad, axis=1, keepdims=True))
            acc[:, start : start + SEQ_LEN] += score_grad
            low = score_grad.astype(BF16)
            out_ref[0, rows, cols] = dot(low, keys).astype(BF16)
            key_part = dot(low, proj_ref[0, rows, cols], ((0,), (0,)))
            value_part = dot(probs.astype(BF16), grad, ((0,), (0,)))
            if j == 0:
                key_acc[...] = key_part
                value_acc[...] = value_part
            else:
                key_acc[...] += key_part
                value_acc[...] += value_part
        out_ref[1, :, cols] = key_acc[...].astype(BF16)
        out_ref[2, :, cols] = value_acc[...].astype(BF16)
        total = acc[...]
        half = TILE // 2
        while half >= 1:
            total = total[:half] + pltpu.roll(total[half : 2 * half], SPAN - half, 1)
            half //= 2
        diag_ref[h : h + 1, :] = total


VMEM = pl.BlockSpec(memory_space=pltpu.VMEM)
SMEM = pl.BlockSpec(memory_space=pltpu.SMEM)


def rms_scale(values):
    return lax.rsqrt(jnp.mean(values * values, axis=-1, keepdims=True) + EPSILON)


def body(
    inputs,
    teacher,
    lengths,
    expert_ids,
    route_slots,
    gain_attn,
    w_qkv,
    w_out,
    rel_table,
    gain_moe,
    w_router,
    w_gate_up,
    w_down,
):
    highest = lax.Precision.HIGHEST
    tok_rows, model_width = inputs.shape
    groups = lax.axis_size("dp")
    shards = lax.axis_size("tensor")
    experts = w_router.shape[1]
    local_experts = w_gate_up.shape[0]
    capacity = 10 * tok_rows // (4 * experts)
    padded_cap = (capacity + 15) // 16 * 16
    slot_count = experts * padded_cap
    heads_here = rel_table.shape[1]
    width_here = w_qkv.shape[2]
    head_width = width_here // heads_here
    share = model_width // shards
    column_start = lax.axis_index("tensor") * share

    def mine(values):
        return lax.dynamic_slice_in_dim(values, column_start, share, values.ndim - 1)

    def gather_columns(values):
        return lax.all_gather(values, "tensor", axis=values.ndim - 1, tiled=True)

    def exchange(values):
        blocks = values.reshape(groups, slot_count // groups, share)
        return lax.all_to_all(blocks, "dp", split_axis=0, concat_axis=0, tiled=True)

    def scatter_columns(values):
        rows = values.shape[0]
        parts = lax.all_to_all(
            values.reshape(rows, shards, share), "tensor", split_axis=1, concat_axis=1, tiled=True
        )
        return jnp.sum(parts.astype(F32), axis=1)

    offsets = jnp.arange(SPAN, dtype=jnp.int32) - SEQ_LEN
    onehot_offsets = bucket_onehot(offsets)
    offset_bias = jnp.dot(onehot_offsets, rel_table, precision=highest).T

    residual = inputs.astype(F32)
    scale_one = rms_scale(residual)
    normed_low = (residual * scale_one * gain_attn).astype(BF16)
    projected = jnp.einsum("td,jde->jte", normed_low, w_qkv, preferred_element_type=F32).astype(BF16)

    attended, probs = pl.pallas_call(
        functools.partial(attention_forward, heads_here, head_width),
        out_shape=(
            jax.ShapeDtypeStruct((tok_rows, width_here), BF16),
            jax.ShapeDtypeStruct((heads_here, SEQ_LEN, SEQ_LEN), F32),
        ),
        in_specs=[SMEM, VMEM, VMEM],
        out_specs=(VMEM, VMEM),
        compiler_params=pltpu.CompilerParams(vmem_limit_bytes=32 * 1024 * 1024),
        name="attention_forward",
    )(lengths, offset_bias, projected)

    w_out_full = lax.all_gather(w_out, "tensor", axis=0, tiled=True)
    attended_full = gather_columns(attended)
    after_attn = residual + jnp.dot(attended_full, w_out_full, preferred_element_type=F32)
    scale_two = rms_scale(after_attn)
    normed_two_low = (after_attn * scale_two * gain_moe).astype(BF16)
    logits = jnp.dot(normed_two_low, w_router, preferred_element_type=F32)
    expert_range = jnp.arange(experts, dtype=jnp.int32)
    picks = (expert_ids[:, :, None] == expert_range[None, None, :]).astype(F32)
    gates, gate_pull = jax.vjp(lambda values: route_gates(values, picks), logits)
    kept_route = route_slots < capacity
    target = jnp.where(kept_route, expert_ids * padded_cap + route_slots, -1)
    slot_range = jnp.arange(slot_count, dtype=jnp.int32)
    route_of = (target[:, :, None] == slot_range[None, None, :]).astype(BF16)
    first_route, second_route = route_of[:, 0], route_of[:, 1]
    any_route = first_route + second_route

    after_mine = mine(after_attn)
    teacher_mine = mine(teacher).astype(F32)
    normed_mine = mine(normed_two_low)
    dispatched = dot(any_route, normed_mine, ((0,), (0,))).astype(BF16)
    expert_rows = gather_columns(exchange(dispatched)).reshape(
        groups, local_experts, padded_cap, model_width
    )
    gate_up = jnp.einsum("nxcd,xjdf->jnxcf", expert_rows, w_gate_up, preferred_element_type=F32)
    activated, gelu_pull = jax.vjp(lambda v: jax.nn.gelu(v, approximate=True), gate_up[0])
    hidden_low = (activated * gate_up[1]).astype(BF16)
    partial_out = jnp.einsum(
        "nxcf,xfd->nxcd", hidden_low, w_down, preferred_element_type=F32
    ).astype(BF16)
    summed = scatter_columns(partial_out.reshape(slot_count, model_width)).astype(BF16)
    returned = exchange(summed).reshape(slot_count, share)
    routed_first = dot(first_route, returned)
    routed_second = dot(second_route, returned)

    row_alive = (jnp.arange(tok_rows, dtype=jnp.int32) < lengths[0]).astype(F32)[:, None]
    valid_total = lax.psum(lengths[0].astype(F32), "dp")
    scale = groups * tok_rows / valid_total
    block_out = after_mine + gates[:, 0, None] * routed_first + gates[:, 1, None] * routed_second
    deviation = (block_out - teacher_mine) * row_alive
    out_grad = deviation * scale
    squared = lax.psum(jnp.sum(deviation * deviation), ("dp", "tensor"))
    loss = squared / (2.0 * valid_total * model_width)

    slot_grad = (
        dot(first_route, (gates[:, 0, None] * out_grad).astype(BF16), ((0,), (0,)))
        + dot(second_route, (gates[:, 1, None] * out_grad).astype(BF16), ((0,), (0,)))
    ).astype(BF16)
    gate_grad_part = jnp.stack(
        [jnp.sum(routed_first * out_grad, axis=-1), jnp.sum(routed_second * out_grad, axis=-1)],
        axis=1,
    )
    gate_grad = lax.psum(gate_grad_part, "tensor")
    expert_grad = gather_columns(exchange(slot_grad)).reshape(
        groups, local_experts, padded_cap, model_width
    )
    down_grad = jnp.einsum("nxcf,nxcd->xfd", hidden_low, expert_grad, preferred_element_type=F32)
    hidden_grad = jnp.einsum("nxcd,xfd->nxcf", expert_grad, w_down, preferred_element_type=F32)
    gate_side = gelu_pull(hidden_grad * gate_up[1])[0]
    up_side = hidden_grad * activated
    pre_grads = jnp.stack([gate_side, up_side], axis=0).astype(BF16)
    gate_up_grad = jnp.einsum(
        "nxcd,jnxcf->xjdf", expert_rows, pre_grads, preferred_element_type=F32
    )
    rows_grad = jnp.einsum("jnxcf,xjdf->nxcd", pre_grads, w_gate_up, preferred_element_type=F32)
    rows_mine = scatter_columns(rows_grad.astype(BF16).reshape(slot_count, model_width))
    back_grad = exchange(rows_mine.astype(BF16)).reshape(slot_count, share)

    logit_grad = gate_pull(gate_grad)[0].astype(BF16)
    router_grad = dot(normed_two_low, logit_grad, ((0,), (0,)))
    normed_two_grad = dot(any_route, back_grad) + mine(dot(logit_grad, w_router, ((1,), (1,))))
    gain_two_mine = mine(gain_moe)

    def rms_back(values, factor, gain, grad):
        projected_part = jnp.sum(grad * gain * values, axis=-1, keepdims=True)
        along = lax.psum(projected_part, "tensor")
        gain_grad = jnp.sum(grad * values * factor, axis=0)
        return factor * (grad * gain - values * (factor * factor * along / model_width)), gain_grad

    after_norm_grad, gain_moe_mine = rms_back(after_mine, scale_two, gain_two_mine, normed_two_grad)
    after_grad = out_grad + after_norm_grad
    branch_grad = gather_columns(after_grad.astype(BF16))
    out_proj_grad = dot(attended, branch_grad, ((0,), (0,)))
    attended_grad = dot(branch_grad, w_out, ((1,), (1,))).astype(BF16)

    projected_grad, diagonals = pl.pallas_call(
        functools.partial(attention_backward, heads_here, head_width),
        out_shape=(
            jax.ShapeDtypeStruct((3, tok_rows, width_here), BF16),
            jax.ShapeDtypeStruct((heads_here, SPAN), F32),
        ),
        in_specs=[VMEM, VMEM, VMEM],
        out_specs=(VMEM, VMEM),
        scratch_shapes=[
            pltpu.VMEM((TILE, SPAN), F32),
            pltpu.VMEM((SEQ_LEN, head_width), F32),
            pltpu.VMEM((SEQ_LEN, head_width), F32),
        ],
        compiler_params=pltpu.CompilerParams(vmem_limit_bytes=32 * 1024 * 1024),
        name="attention_backward",
    )(projected, probs, attended_grad)
    table_grad = jnp.dot(onehot_offsets.T, diagonals.T, precision=highest)

    qkv_grad = jnp.einsum("td,jte->jde", normed_low, projected_grad, preferred_element_type=F32)
    normed_one_part = jnp.einsum("jte,jde->td", projected_grad, w_qkv, preferred_element_type=F32)
    normed_one_grad = scatter_columns(normed_one_part.astype(BF16))
    input_norm_grad, gain_attn_mine = rms_back(
        mine(residual), scale_one, mine(gain_attn), normed_one_grad
    )
    input_grad = after_grad + input_norm_grad

    def place(part):
        whole = jnp.zeros((model_width,), F32)
        return lax.dynamic_update_slice_in_dim(whole, part, column_start, 0)

    gains = lax.psum(jnp.stack([place(gain_attn_mine), place(gain_moe_mine)]), ("dp", "tensor"))
    router_sum = lax.psum(router_grad.astype(BF16), "dp").astype(F32)
    qkv_sum = lax.psum(qkv_grad.astype(BF16), "dp").astype(F32)
    out_proj_sum = lax.psum(out_proj_grad.astype(BF16), "dp").astype(F32)
    table_sum = lax.psum(table_grad, "dp")
    return (
        block_out,
        loss,
        input_grad,
        gains[0],
        qkv_sum,
        out_proj_sum,
        table_sum,
        gains[1],
        router_sum,
        gate_up_grad,
        down_grad,
    )


def solution(mesh):
    placed = (
        P("dp", None),
        P("dp", None),
        P("dp"),
        P("dp", None),
        P("dp", None),
        P(),
        P(None, None, "tensor"),
        P("tensor", None),
        P(None, "tensor"),
        P(),
        P(),
        P("dp", None, None, "tensor"),
        P("dp", "tensor", None),
    )
    return jax.shard_map(
        body,
        mesh=mesh,
        in_specs=placed,
        out_specs=(
            P("dp", "tensor"),
            P(),
            P("dp", "tensor"),
            P(),
            P(None, None, "tensor"),
            P("tensor", None),
            P(None, "tensor"),
            P(),
            P(),
            P("dp", None, None, "tensor"),
            P("dp", "tensor", None),
        ),
        check_vma=False,
    )
```

time: 1760 us -> 552 us (0.31); the launches traced: 1730 us -> 545 us
  local copies, waits for them, and re-layouts: 1130 us -> 33.2 us
  blocking collectives: 268 us -> 179 us
  other arithmetic: 41.2 us -> 20 us
    gather x2 -> x0, local copies, waits for them, and re-layouts: 1020 us -> none  [block_view(): bias = jnp.take(offset_bias, lookup, axis=1)]
    psum x5 -> x1, waiting for transfers between devices: 127 us -> 27.2 us  [body(): qkv_sum = lax.psum(qkv_grad.astype(BF16), 'dp').astype(F32)]
    all_gather x0 -> x5, waiting for transfers between devices: none -> 88.2 us  [the longest x4 64 us: gather_columns(): return lax.all_gather(values, 'tensor', axis=values.ndim - 1, tiled=True)]
    all_to_all x2, blocking collectives: 130 us -> 45.7 us  [exchange(): return lax.all_to_all(blocks, 'dp', split_axis=0, concat_axis=0, tiled=True)]
    rev x1 -> x0, local copies, waits for them, and re-layouts: 34.8 us -> none  [diagonal_sums(): flipped = score_grad[:, ::-1, :]]
    unnamed x105 -> x57, local copies, waits for them, and re-layouts: 39.5 us -> 12 us
    dot_general x21 -> x17, matrix products: 43.8 us -> 29.6 us  [the longest x10 16.9 us: dot(): return lax.dot_general(a, b, (dims, ((), ())), preferred_element_type=F32)]
    all_to_all x2 -> x5, waiting for transfers between devices: 56.8 us -> 64.5 us  [the longest x3 40 us: scatter_columns(): lax.all_to_all(values.reshape(rows, shards, share), 'tensor', split_axis=...]
  transfers between devices with their start and end apart: 7 -> 11, of which waited for: 4 -> 9; matrix products, arithmetic and copies ran while one was open for 8% -> 6% of each run, Pallas kernels for 0% -> 0%
where the time goes in v1:
time: 552 us; the launch traced here: 545 us
  waiting for transfers between devices  181 us (33%)
  blocking collectives  179 us (32%)
  matrix products  75.6 us (14%)
  local copies, waits for them, and re-layouts  33.2 us (6%)
  starting transfers between devices  24 us (4%)
  other arithmetic  20 us (4%)
  between operations  18.8 us (3%)
  Pallas kernels  14.2 us (3%)
    all_gather x4, waiting for transfers between devices, gather_columns(): return lax.all_gather(values, 'tensor', axis=values.ndim - 1, tiled=True)  64 us
    all_to_all x2, blocking collectives, exchange(): return lax.all_to_all(blocks, 'dp', split_axis=0, concat_axis=0, tiled=True)  45.7 us
    all_to_all x3, waiting for transfers between devices, scatter_columns(): lax.all_to_all(values.reshape(rows, shards, share), 'tensor', split_axis=...  40 us
    psum x1, blocking collectives, body(): squared = lax.psum(jnp.sum(deviation * deviation), ('dp', 'tensor'))  38.9 us
    psum x1, blocking collectives, body(): router_sum = lax.psum(router_grad.astype(BF16), 'dp').astype(F32)  35.7 us
    psum x1, waiting for transfers between devices, body(): qkv_sum = lax.psum(qkv_grad.astype(BF16), 'dp').astype(F32)  27.2 us
    all_to_all x2, waiting for transfers between devices, exchange(): return lax.all_to_all(blocks, 'dp', split_axis=0, concat_axis=0, tiled=True)  24.6 us
    all_gather x1, waiting for transfers between devices, body(): w_out_full = lax.all_gather(w_out, 'tensor', axis=0, tiled=True)  24.2 us
  transfers between devices with their start and end apart: 11, of which 9 were waited for; matrix products, arithmetic and copies ran while one was open for 6% of the time, Pallas kernels for 0%

profile of v1, /device:TPU:0, one launch (start us, length us, event | category | flops | bytes accessed | tf_op | source)
XLA Modules:
  0.0 545.0 jit_solution(13988137055439871934)
XLA Ops:
  8.1 1.5 multiply_reduce_fusion.1
  9.6 1.1 convolution_bitcast_fusion.2.bias_ref
  10.7 2.8 fusion.36.proj_ref
  13.5 6.6 %attention_forward.1 = (bf16[512,256]{1,0:T(8,128)(2,1)}, f32[4,512,512]{2,1,0:T(8,128)S(1)}) custom-call(s32[1]{0:T(128)} %copy.140.len_ref, f32[4,1024]{1,0:T(4,128)S(1)} %convolution_bitcast_fusion.2.bias_ref, bf16[3,512,256]{2,1,0:T(8,128)(2,1)S(1)} %fusion.36.proj_ref), custom_call_target="tpu_custom_call" | custom-call | tf_op jit(solution)/shard_map/attention_forward/pallas_call | solution.py:166
  20.1 2.0 copy-done.2
  23.0 2.5 iota_compare_fusion
  25.5 16.4 %all-gather.6.cloned.1.call-done = bf16[512,1024]{1,0:T(8,128)(2,1)} async-done(((bf16[512,256]{1,0:T(8,128)(2,1)}), bf16[512,1024]{1,0:T(8,128)(2,1)}) %all-gather.6.cloned.1.call-update) | async-done | bytes 1048592 | tf_op jit(solution)/shard_map/all_gather | solution.py:144
  41.9 24.2 %all-gather.8.cloned.1.call-done = bf16[1024,1024]{1,0:T(8,128)(2,1)} async-done(((bf16[256,1024]{1,0:T(8,128)(2,1)}), bf16[1024,1024]{1,0:T(8,128)(2,1)}) %all-gather.8.cloned.1.call-update) | async-done | bytes 2097168 | tf_op jit(solution)/shard_map/all_gather | solution.py:178
  66.1 3.5 multiply_reduce_fusion
  70.8 1.6 copy-done.13
  73.1 23.8 %all_to_all.35 = bf16[8,160,256]{2,1,0:T(8,128)(2,1)} all-to-all(bf16[8,160,256]{2,1,0:T(8,128)(2,1)S(1)} %bitcast.175), channel_id=1, replica_groups=mesh['dp'=8,'tensor'=4] {'dp'}, dimensions={0} | all-to-all | bytes 1310720 | tf_op jit(solution)/shard_map/all_to_all | solution.py:148
  96.9 23.8 %all-gather.10.cloned.1.call-done = bf16[8,160,1024]{2,1,0:T(8,128)(2,1)} async-done(((bf16[8,160,256]{2,1,0:T(8,128)(2,1)}), bf16[8,160,1024]{2,1,0:T(8,128)(2,1)}) %all-gather.10.cloned.1.call-update) | async-done | bytes 2621456 | tf_op jit(solution)/shard_map/all_gather | solution.py:144
  120.7 7.1 %fusion.14 = f32[2,8,2,80,704]{4,3,0,1,2:T(8,128)S(1)} fusion(bf16[2,2,1024,704]{2,3,1,0:T(8,128)(2,1)} %param.24, bf16[8,2,80,1024,1]{3,2,1,0,4:T(8,128)(2,1)} %bitcast.192), kind=kOutput, calls=%fused_computation.26 | convolution fusion | flops 3690987520 | bytes 15597568 | tf_op jit(solution)/shard_map/nxcd,xjdf->jnxcf/dot_general | solution.py:201
  127.8 1.4 multiply_convert_fusion
  129.2 1.8 copy-done.8
  131.0 2.2 convert_bitcast_fusion
  133.3 1.9 copy.77
  135.2 5.5 %reshape_reshape.6 = bf16[1280,4,256]{2,1,0:T(4,128)(2,1)} reshape(bf16[8,2,80,1024]{3,2,1,0:T(8,128)(2,1)} %copy.77) | data formatting | bytes 5242880 | tf_op jit(solution)/shard_map/reshape;reshape | solution.py:153
  140.7 3.6 copy.78
  144.3 4.5 all-to-all-start.1
  148.9 21.9 %psum.71 = f32[]{:T(128)} all-reduce(f32[]{:T(128)S(6)} %convert_element_type.182), channel_id=1, replica_groups=mesh['dp'=8,'tensor'=4] {'dp'}, use_global_device_ids=true, to_apply=%region_9.10 | all-reduce | flops 1 | bytes 8 | tf_op jit(solution)/shard_map/psum | solution.py:213
  171.5 8.8 %all-to-all-done.1 = bf16[1280,4,256]{2,0,1:T(8,128)(2,1)} async-done(((bf16[1280,4,256]{2,0,1:T(8,128)(2,1)}), bf16[1280,4,256]{2,0,1:T(8,128)(2,1)}, u32[]{:S(2)}, u32[]{:S(2)}) %all-to-all-start.1) | async-done | bytes 2621472 | tf_op jit(solution)/shard_map/all_to_all | solution.py:152
  180.2 3.2 reduce_sum.185
  183.4 5.5 %all-to-all-start.2 = ((bf16[8,160,256]{2,1,0:T(8,128)(2,1)}), bf16[8,160,256]{2,1,0:T(8,128)(2,1)}, u32[]{:S(2)}, u32[]{:S(2)}) async-start(bf16[8,160,256]{2,1,0:T(8,128)(2,1)} %bitcast.17), calls=%async_computation.2 | async-start | bytes 1310720 | tf_op jit(solution)/shard_map/all_to_all | solution.py:148
  189.0 1.6 fusion.70
  190.7 15.4 %all-to-all-done.2 = bf16[8,160,256]{2,1,0:T(8,128)(2,1)} async-done(((bf16[8,160,256]{2,1,0:T(8,128)(2,1)}), bf16[8,160,256]{2,1,0:T(8,128)(2,1)}, u32[]{:S(2)}, u32[]{:S(2)}) %all-to-all-start.2) | async-done | bytes 655392 | tf_op jit(solution)/shard_map/all_to_all | solution.py:148
  206.1 2.0 fusion.31
  208.1 3.6 multiply_reduce_fusion.7
  212.7 1.0 fusion.24
  213.8 21.9 %all_to_all.36 = bf16[8,160,256]{2,1,0:T(8,128)(2,1)} all-to-all(bf16[8,160,256]{2,1,0:T(8,128)(2,1)S(1)} %bitcast.174), channel_id=1, replica_groups=mesh['dp'=8,'tensor'=4] {'dp'}, dimensions={0} | all-to-all | bytes 1310720 | tf_op jit(solution)/shard_map/all_to_all | solution.py:148
  235.7 23.8 %all-gather.12.cloned.1.call-done = bf16[8,160,1024]{2,1,0:T(8,128)(2,1)} async-done(((bf16[8,160,256]{2,1,0:T(8,128)(2,1)}), bf16[8,160,1024]{2,1,0:T(8,128)(2,1)}) %all-gather.12.cloned.1.call-update) | async-done | bytes 2621456 | tf_op jit(solution)/shard_map/all_gather | solution.py:144
  259.5 8.4 %fusion.33 = (bf16[1,8,2,80,704]{4,3,1,2,0:T(8,128)(2,1)S(1)}, bf16[1,8,2,80,704]{4,3,1,2,0:T(8,128)(2,1)S(1)}) fusion(f32[2,8,2,80,704]{4,3,0,1,2:T(8,128)} %copy-done.8, bf16[2,704,1024]{2,1,0:T(8,128)(2,1)S(1)} %copy-done, bf16[8,2,80,1024]{3,2,1,0:T(8,128)(2,1)} %bitcast.194), kind=kOutput, calls=%fused_computation.53 | convolution fusion | flops 1867120640 | bytes 16318464 | tf_op jit(solution)/shard_map/nxcd,xfd->nxcf/dot_general | solution.py:234
  267.9 8.5 %fusion.2 = bf16[2,8,80,1024,1]{3,2,0,1,4:T(8,128)(2,1)S(1)} fusion(bf16[2,2,1024,704]{2,3,1,0:T(8,128)(2,1)} %param.24, bf16[1,8,2,80,704]{4,3,1,2,0:T(8,128)(2,1)S(1)} %get-tuple-element.81, bf16[1,8,2,80,704]{4,3,1,2,0:T(8,128)(2,1)S(1)} %get-tuple-element.80), kind=kOutput, calls=%fused_computation.2 | convolution fusion | flops 3692789760 | bytes 11993088 | tf_op jit(solution)/shard_map/jnxcf,xjdf->nxcd/dot_general | solution.py:241
  276.8 1.8 copy.83
  278.6 4.3 reshape_reshape.7
  283.0 1.8 copy.84
  284.8 3.7 all-to-all-start.4
  288.5 31.2 %all-to-all-done.4 = bf16[1280,4,256]{2,0,1:T(8,128)(2,1)S(1)} async-done(((bf16[1280,4,256]{2,0,1:T(8,128)(2,1)}), bf16[1280,4,256]{2,0,1:T(8,128)(2,1)S(1)}, u32[]{:S(2)}, u32[]{:S(2)}) %all-to-all-start.4) | async-done | bytes 2621472 | tf_op jit(solution)/shard_map/all_to_all | solution.py:152
  319.7 1.4 reduce_sum.187
  321.1 5.8 %all-to-all-start.5 = ((bf16[8,160,256]{2,1,0:T(8,128)(2,1)}), bf16[8,160,256]{2,1,0:T(8,128)(2,1)}, u32[]{:S(2)}, u32[]{:S(2)}) async-start(bf16[8,160,256]{2,1,0:T(8,128)(2,1)} %bitcast.31), calls=%async_computation.5 | async-start | bytes 1310720 | tf_op jit(solution)/shard_map/all_to_all | solution.py:148
  327.0 6.1 %psum.72 = f32[512,2]{0,1:T(2,128)S(1)} all-reduce(f32[512,2]{0,1:T(2,128)S(1)} %pad_maximum_fusion.2), channel_id=1, replica_groups=mesh['dp'=8,'tensor'=4] {'tensor'}, use_global_device_ids=true, to_apply=%region_13.14 | all-reduce | flops 1024 | bytes 8192 | tf_op jit(solution)/shard_map/psum | solution.py:229
  333.2 1.8 fusion.75
  335.0 9.2 %all-to-all-done.5 = bf16[8,160,256]{2,1,0:T(8,128)(2,1)} async-done(((bf16[8,160,256]{2,1,0:T(8,128)(2,1)}), bf16[8,160,256]{2,1,0:T(8,128)(2,1)}, u32[]{:S(2)}, u32[]{:S(2)}) %all-to-all-start.5) | async-done | bytes 655392 | tf_op jit(solution)/shard_map/all_to_all | solution.py:148
  344.1 2.7 multiply_reduce_fusion.2
  346.8 5.8 %psum.73 = f32[512,1]{0,1:T(1,128)S(1)} all-reduce(f32[512,1]{0,1:T(1,128)S(1)} %bitcast.184), channel_id=1, replica_groups=mesh['dp'=8,'tensor'=4] {'tensor'}, use_global_device_ids=true, to_apply=%region_18.19 | all-reduce | flops 512 | bytes 4096 | tf_op jit(solution)/shard_map/psum | solution.py:252
  352.6 2.4 fusion.67
  355.1 1.6 convert_element_type.163
  357.6 35.7 %psum.79 = bf16[1024,16]{0,1:T(8,128)(2,1)S(1)} all-reduce(bf16[1024,16]{0,1:T(8,128)(2,1)S(1)} %convolution_convert_fusion.5), channel_id=1, replica_groups=mesh['dp'=8,'tensor'=4] {'dp'}, use_global_device_ids=true, to_apply=%region_28.29 | all-reduce | flops 16384 | bytes 65536 | tf_op jit(solution)/shard_map/psum | solution.py:293
  394.0 12.1 %convolution_bitcast_fusion = f32[2,2,1024,704]{2,3,1,0:T(8,128)} fusion(bf16[8,2,80,1024,1]{3,2,1,0,4:T(8,128)(2,1)} %bitcast.193, bf16[1,8,2,80,704]{4,3,1,2,0:T(8,128)(2,1)} %copy-done.27, bf16[1,8,2,80,704]{4,3,1,2,0:T(8,128)(2,1)} %copy-done.26), kind=kOutput, calls=%fused_computation.8 | convolution fusion | flops 3692789760 | bytes 17760256 | tf_op jit(solution)/shard_map/nxcd,jnxcf->xjdf/dot_general | solution.py:238
  406.1 1.7 convolution_convert_fusion.4.grad_ref
  407.8 2.2 copy-done.3
  410.0 7.6 %attention_backward.1 = (bf16[3,512,256]{2,1,0:T(8,128)(2,1)S(1)}, f32[4,1024]{1,0:T(4,128)S(1)}) custom-call(bf16[3,512,256]{2,1,0:T(8,128)(2,1)S(1)} %copy-done.5, f32[4,512,512]{2,1,0:T(8,128)S(1)} %copy-done.3, bf16[512,256]{1,0:T(8,128)(2,1)S(1)} %convolution_convert_fusion.4.grad_ref), custom_call_target="tpu_custom_call" | custom-call | tf_op jit(solution)/shard_map/attention_backward/pallas_call | solution.py:262
  418.9 2.5 fusion.34
  421.4 1.0 copy.134
  422.4 4.2 all-to-all-start.6
  426.7 2.2 convolution_convert_fusion.3
  429.0 7.5 %convolution_bitcast_fusion.1 = f32[2,704,1024]{2,1,0:T(8,128)} fusion(bf16[8,2,80,704]{3,2,0,1:T(8,128)(2,1)} %copy-done.15, bf16[8,2,80,1024]{3,2,1,0:T(8,128)(2,1)} %bitcast.195), kind=kOutput, calls=%fused_computation.40 | convolution fusion | flops 1845493760 | bytes 10190848 | tf_op jit(solution)/shard_map/nxcf,nxcd->xfd/dot_general | solution.py:233
  436.8 18.7 %psum.78 = f32[32,4]{0,1:T(4,128)} all-reduce(f32[32,4]{0,1:T(4,128)S(1)} %fusion.40), channel_id=1, replica_groups=mesh['dp'=8,'tensor'=4] {'dp'}, use_global_device_ids=true, to_apply=%region_27.28 | all-reduce | flops 128 | bytes 1024 | tf_op jit(solution)/shard_map/psum | solution.py:296
  455.5 1.4 convert_reduce_fusion
  457.2 38.9 %all-reduce = (f32[]{:T(128)}, f32[2,1024]{1,0:T(2,128)S(1)}) all-reduce(f32[]{:T(128)} %get-tuple-element.69, f32[2,1024]{1,0:T(2,128)S(1)} %pad_maximum_fusion.1), channel_id=1, replica_groups=mesh['dp'=8,'tensor'=4] {'dp','tensor'}, use_global_device_ids=true, to_apply=%region_8.9 | all-reduce | flops 2049 | bytes 16392 | tf_op jit(solution)/shard_map/psum | solution.py:218
  496.8 5.8 %psum.74 = f32[512,1]{0,1:T(1,128)S(1)} all-reduce(f32[512,1]{0,1:T(1,128)S(1)} %bitcast.176), channel_id=1, replica_groups=mesh['dp'=8,'tensor'=4] {'tensor'}, use_global_device_ids=true, to_apply=%region_21.22 | all-reduce | flops 512 | bytes 4096 | tf_op jit(solution)/shard_map/psum | solution.py:252
  504.2 27.2 %all-reduce.4.cloned.1.call-done = (bf16[3,1024,256]{1,2,0:T(8,128)(2,1)}, bf16[256,1024]{1,0:T(8,128)(2,1)}) async-done(((bf16[3,1024,256]{1,2,0:T(8,128)(2,1)}, bf16[256,1024]{1,0:T(8,128)(2,1)}), (bf16[3,1024,256]{1,2,0:T(8,128)(2,1)}, bf16[256,1024]{1,0:T(8,128)(2,1)})) %all-reduce.4.cloned.1.call-update) | async-done | bytes 2097168 | tf_op jit(solution)/shard_map/psum | solution.py:294
  531.5 2.3 convert_element_type.197
  533.7 3.1 copy.92
  (106 shorter events, 9.1 us)
Async XLA Ops:
  7.2 123.8 %copy-start = (bf16[2,704,1024]{2,1,0:T(8,128)(2,1)S(1)}, bf16[2,704,1024]{2,1,0:T(8,128)(2,1)}, u32[]{:S(2)}) copy-start(bf16[2,704,1024]{2,1,0:T(8,128)(2,1)} %param.25) | copy-start | bytes 8650756
  7.2 34.7 %all-gather.6.cloned.1.call-start = ((), (), s32[]{:S(2)}) async-start(), calls=%async_computation.7 | async-start | bytes 1310720 | tf_op jit(solution)/shard_map/all_gather | solution.py:144
  10.7 12.3 %copy-start.21 = (s32[512,2]{0,1:T(2,128)S(1)}, s32[512,2]{0,1:T(2,128)}, u32[]{:S(2)}) copy-start(s32[512,2]{0,1:T(2,128)} %param.16) | copy-start | bytes 12292
  10.7 12.3 %copy-start.23 = (s32[512,2]{0,1:T(2,128)S(1)}, s32[512,2]{0,1:T(2,128)}, u32[]{:S(2)}) copy-start(s32[512,2]{0,1:T(2,128)} %param.17) | copy-start | bytes 12292
  13.5 6.6 %copy-start.4 = (bf16[3,512,256]{2,1,0:T(8,128)(2,1)}, bf16[3,512,256]{2,1,0:T(8,128)(2,1)S(1)}, u32[]{:S(2)}) copy-start(bf16[3,512,256]{2,1,0:T(8,128)(2,1)S(1)} %fusion.36.proj_ref) | copy-start | bytes 2359300
  20.1 2.0 copy-start.2
  22.2 43.9 %all-gather.8.cloned.1.call-start = ((), (), s32[]{:S(2)}) async-start(), calls=%async_computation.8 | async-start | bytes 2621440 | tf_op jit(solution)/shard_map/all_gather | solution.py:178
  22.9 97.7 %all-gather.10.cloned.1.call-start = ((), (), s32[]{:S(2)}) async-start(), calls=%async_computation.9 | async-start | bytes 3276800 | tf_op jit(solution)/shard_map/all_gather | solution.py:144
  25.5 44.1 %copy-start.22 = (f32[1024]{0:T(1024)S(1)}, f32[1024]{0:T(1024)}, u32[]{:S(2)}) copy-start(f32[1024]{0:T(1024)} %param.22) | copy-start | bytes 12292
  69.6 3.5 copy-start.12
  69.6 2.9 copy-start.13
  69.9 1.0 copy-start.6
  127.8 3.2 copy-start.8
  131.0 2.3 copy-start.15
  144.3 35.9 %all-to-all-start.1 = ((bf16[1280,4,256]{2,0,1:T(8,128)(2,1)}), bf16[1280,4,256]{2,0,1:T(8,128)(2,1)}, u32[]{:S(2)}, u32[]{:S(2)}) async-start(bf16[1280,4,256]{2,0,1:T(8,128)(2,1)} %copy.78), calls=%async_computation.1 | async-start | bytes 5242880 | tf_op jit(solution)/shard_map/all_to_all | solution.py:152
  148.9 40.1 %copy-start.20 = (bf16[1024,16]{0,1:T(8,128)(2,1)S(1)}, bf16[1024,16]{0,1:T(8,128)(2,1)}, u32[]{:S(2)}) copy-start(bf16[1024,16]{0,1:T(8,128)(2,1)} %param.23) | copy-start | bytes 98308
  183.4 22.7 %all-to-all-start.2 = ((bf16[8,160,256]{2,1,0:T(8,128)(2,1)}), bf16[8,160,256]{2,1,0:T(8,128)(2,1)}, u32[]{:S(2)}, u32[]{:S(2)}) async-start(bf16[8,160,256]{2,1,0:T(8,128)(2,1)} %bitcast.17), calls=%async_computation.2 | async-start | bytes 1310720 | tf_op jit(solution)/shard_map/all_to_all | solution.py:148
  188.9 70.6 %all-gather.12.cloned.1.call-start = ((), (), s32[]{:S(2)}) async-start(), calls=%async_computation.10 | async-start | bytes 3276800 | tf_op jit(solution)/shard_map/all_gather | solution.py:144
  206.1 2.0 copy-start.16
  211.7 2.0 copy-start.19
  267.9 8.5 %copy-start.26 = (bf16[1,8,2,80,704]{4,3,1,2,0:T(8,128)(2,1)}, bf16[1,8,2,80,704]{4,3,1,2,0:T(8,128)(2,1)S(1)}, u32[]{:S(2)}) copy-start(bf16[1,8,2,80,704]{4,3,1,2,0:T(8,128)(2,1)S(1)} %get-tuple-element.80) | copy-start | bytes 5406724
  267.9 8.5 %copy-start.27 = (bf16[1,8,2,80,704]{4,3,1,2,0:T(8,128)(2,1)}, bf16[1,8,2,80,704]{4,3,1,2,0:T(8,128)(2,1)S(1)}, u32[]{:S(2)}) copy-start(bf16[1,8,2,80,704]{4,3,1,2,0:T(8,128)(2,1)S(1)} %get-tuple-element.81) | copy-start | bytes 5406724
  284.8 34.9 %all-to-all-start.4 = ((bf16[1280,4,256]{2,0,1:T(8,128)(2,1)}), bf16[1280,4,256]{2,0,1:T(8,128)(2,1)S(1)}, u32[]{:S(2)}, u32[]{:S(2)}) async-start(bf16[1280,4,256]{2,0,1:T(8,128)(2,1)} %copy.84), calls=%async_computation.4 | async-start | bytes 5242880 | tf_op jit(solution)/shard_map/all_to_all | solution.py:152
  321.1 23.0 %copy-start.14 = (bf16[512,2,1280]{2,0,1:T(8,128)(2,1)S(1)}, bf16[512,2,1280]{2,0,1:T(8,128)(2,1)}, u32[]{:S(2)}) copy-start(bf16[512,2,1280]{2,0,1:T(8,128)(2,1)} %get-tuple-element.87) | copy-start | bytes 7864324
  321.1 23.0 %all-to-all-start.5 = ((bf16[8,160,256]{2,1,0:T(8,128)(2,1)}), bf16[8,160,256]{2,1,0:T(8,128)(2,1)}, u32[]{:S(2)}, u32[]{:S(2)}) async-start(bf16[8,160,256]{2,1,0:T(8,128)(2,1)} %bitcast.31), calls=%async_computation.5 | async-start | bytes 1310720 | tf_op jit(solution)/shard_map/all_to_all | solution.py:148
  326.9 79.2 %all-gather.14.cloned.1.call-start = ((), (), s32[]{:S(2)}) async-start(), calls=%async_computation.11 | async-start | bytes 1310720 | tf_op jit(solution)/shard_map/all_gather | solution.py:144
  346.8 8.2 %copy-start.24 = (f32[1024]{0:T(1024)S(1)}, f32[1024]{0:T(1024)}, u32[]{:S(2)}) copy-start(f32[1024]{0:T(1024)} %param.18) | copy-start | bytes 12292
  346.8 8.3 %copy-start.10 = (bf16[512,1024]{1,0:T(8,128)(2,1)S(1)}, bf16[512,1024]{1,0:T(8,128)(2,1)}, u32[]{:S(2)}) copy-start(bf16[512,1024]{1,0:T(8,128)(2,1)} %param.13) | copy-start | bytes 3145732
  352.6 4.7 copy-start.7
  394.0 12.2 %copy-start.18 = (bf16[256,1024]{1,0:T(8,128)(2,1)S(1)}, bf16[256,1024]{1,0:T(8,128)(2,1)}, u32[]{:S(2)}) copy-start(bf16[256,1024]{1,0:T(8,128)(2,1)} %param.20) | copy-start | bytes 1572868
  394.0 13.9 %copy-start.5 = (bf16[3,512,256]{2,1,0:T(8,128)(2,1)S(1)}, bf16[3,512,256]{2,1,0:T(8,128)(2,1)}, u32[]{:S(2)}) copy-start(bf16[3,512,256]{2,1,0:T(8,128)(2,1)} %copy-done.4) | copy-start | bytes 2359300
  407.8 2.2 copy-start.3
  410.0 7.6 %copy-start.25 = (bf16[3,1024,256]{2,1,0:T(8,128)(2,1)S(1)}, bf16[3,1024,256]{2,1,0:T(8,128)(2,1)}, u32[]{:S(2)}) copy-start(bf16[3,1024,256]{2,1,0:T(8,128)(2,1)} %param.19) | copy-start | bytes 4718596
  417.6 1.2 copy-start.11
  421.4 5.3 copy-start.17
  422.4 33.1 %all-to-all-start.6 = ((bf16[512,4,256]{2,0,1:T(8,128)(2,1)}), bf16[512,4,256]{2,0,1:T(8,128)(2,1)}, u32[]{:S(2)}, u32[]{:S(2)}) async-start(bf16[512,4,256]{2,0,1:T(8,128)(2,1)} %bitcast.169), calls=%async_computation.6 | async-start | bytes 2097152 | tf_op jit(solution)/shard_map/all_to_all | solution.py:152
  426.7 104.8 %all-reduce.4.cloned.1.call-start = ((), (), s32[]{:S(2)}) async-start(), calls=%async_computation.12 | async-start | bytes 4194304 | tf_op jit(solution)/shard_map/psum | solution.py:294
  429.0 28.0 %copy-start.9 = (f32[512,1024]{1,0:T(8,128)S(1)}, f32[512,1024]{1,0:T(8,128)}, u32[]{:S(2)}) copy-start(f32[512,1024]{1,0:T(8,128)} %convert_element_type.163) | copy-start | bytes 6291460
  531.5 5.3 copy-start.1
Sparse Core Ops, SparseCore 0:
  22.3 19.5 all-gather.5
  43.4 22.5 all-gather.7
  97.0 23.6 all-gather.9
  235.8 23.6 all-gather.11
  355.2 16.1 all-gather.13
  430.8 100.5 all-reduce.3

commit v2 on v1

--- a/solution.py
+++ b/solution.py
@@ -103,6 +103,300 @@
 SMEM = pl.BlockSpec(memory_space=pltpu.SMEM)
 
 
+MESH_ID = pl.DeviceIdType.MESH
+ANY = pl.BlockSpec(memory_space=pl.ANY)
+
+
+class Mover:
+    def __init__(self, groups, shards, cap, chunk, source, rows, part, back, scratch):
+        self.groups, self.lines, self.cap, self.chunk = groups, shards // 2, cap, chunk
+        self.source, self.rows, self.part, self.back = source, rows, part, back
+        (self.mate_in, self.line_out, self.line_in, self.back_out, self.dp_sems, self.row_sems, self.sum_sems) = scratch
+        self.me, self.place = lax.axis_index("dp"), lax.axis_index("tensor")
+        self.line, self.core = lax.div(self.place, 2), lax.rem(self.place, 2)
+        self.steps = groups // chunk
+
+    def group(self, offset):
+        return lax.rem(self.me + offset, self.groups)
+
+    def shard(self, offset, core):
+        return lax.rem(self.line + offset, self.lines) * 2 + core
+
+    def greet(self):
+        barrier = pltpu.get_barrier_semaphore()
+        for i in range(1, self.groups):
+            pl.semaphore_signal(barrier, inc=1, device_id={"dp": self.group(i)}, device_id_type=MESH_ID)
+        for d in range(1, self.lines):
+            pl.semaphore_signal(barrier, inc=1, device_id={"tensor": self.shard(d, self.core)}, device_id_type=MESH_ID)
+        pl.semaphore_signal(barrier, inc=1, device_id={"tensor": self.shard(0, 1 - self.core)}, device_id_type=MESH_ID)
+        pl.semaphore_wait(barrier, self.groups - 1 + self.lines)
+
+    def remote(self, src, dst, sems, index, device):
+        return pltpu.make_async_remote_copy(
+            src_ref=src, dst_ref=dst, send_sem=sems.at[(0, *index)], recv_sem=sems.at[(1, *index)],
+            device_id=device, device_id_type=MESH_ID,
+        )
+
+    def here(self, shard, i):
+        return self.rows.at[shard, :, pl.ds(i * self.cap, self.cap), :]
+
+    def send_out(self):
+        pltpu.make_async_copy(self.source.at[self.me], self.here(self.place, 0), self.dp_sems.at[0, 1, 0]).start()
+        for i in range(1, self.groups):
+            self.out_copy(i).start()
+
+    def out_copy(self, i):
+        to = self.group(i)
+        return self.remote(self.source.at[to], self.here(self.place, i), self.dp_sems.at[0], (i,), {"dp": to})
+
+    def line_copy(self, d, i):
+        return self.remote(
+            self.here(self.place, i), self.here(self.place, i), self.row_sems.at[0], (d, i),
+            {"tensor": self.shard(d, self.core)},
+        )
+
+    def mate_copy(self, d, i):
+        shard = self.shard(self.lines - d, self.core)
+        return self.remote(
+            self.here(shard, i), self.here(shard, i), self.row_sems.at[1], (d, i),
+            {"tensor": self.shard(0, 1 - self.core)},
+        )
+
+    def landed(self, where, sems, index):
+        self.remote(where, where, sems, index, {"tensor": self.shard(0, 1 - self.core)}).wait_recv()
+
+    def places(self, k):
+        return range(k * self.chunk, (k + 1) * self.chunk)
+
+    def spread(self, k):
+        for i in self.places(k):
+            where = self.here(self.place, i)
+            if i == 0:
+                pltpu.make_async_copy(self.source.at[self.me], where, self.dp_sems.at[0, 1, 0]).wait()
+            else:
+                self.landed(where, self.dp_sems.at[0], (i,))
+            for d in range(1, self.lines):
+                self.line_copy(d, i).start()
+            self.mate_copy(0, i).start()
+
+    def relay(self, k):
+        for i in self.places(k):
+            for d in range(1, self.lines):
+                shard = self.shard(self.lines - d, self.core)
+                self.landed(self.here(shard, i), self.row_sems.at[0], (d, i))
+                self.mate_copy(d, i).start()
+
+    def collect(self, k):
+        for i in self.places(k):
+            for d in range(self.lines):
+                shard = self.shard(self.lines - d, 1 - self.core)
+                self.landed(self.here(shard, i), self.row_sems.at[1], (d, i))
+
+    def span(self, k):
+        return pl.ds(k * self.chunk * self.cap, self.chunk * self.cap)
+
+    def pair_copy(self, d, k):
+        shard = self.shard(d, 1 - self.core)
+        return self.remote(
+            self.part.at[shard, :, self.span(k), :], self.mate_in.at[d, :, self.span(k), :], self.sum_sems.at[0], (d, k),
+            {"tensor": self.shard(0, 1 - self.core)},
+        )
+
+    def sum_copy(self, d, k):
+        return self.remote(
+            self.line_out.at[d, :, self.span(k), :], self.line_in.at[d, :, self.span(k), :], self.sum_sems.at[1], (d, k),
+            {"tensor": self.shard(d, self.core)},
+        )
+
+    def back_copy(self, i):
+        return self.remote(
+            self.back_out.at[:, pl.ds(i * self.cap, self.cap), :], self.back.at[self.me], self.dp_sems.at[1], (i,),
+            {"dp": self.group(self.groups - i)},
+        )
+
+    def pair(self, k):
+        for d in range(self.lines):
+            self.pair_copy(d, k).start()
+
+    def pair_sum(self, d, k):
+        shard = self.shard(d, self.core)
+        return self.part[shard, :, self.span(k), :].astype(F32) + self.mate_in[d, :, self.span(k), :].astype(F32)
+
+    def along(self, k):
+        for d in range(self.lines):
+            self.landed(self.mate_in.at[d, :, self.span(k), :], self.sum_sems.at[0], (d, k))
+        for d in range(1, self.lines):
+            self.line_out[d, :, self.span(k), :] = self.pair_sum(d, k).astype(BF16)
+            self.sum_copy(d, k).start()
+
+    def give(self, k):
+        total = self.pair_sum(0, k)
+        for d in range(1, self.lines):
+            self.landed(self.line_in.at[d, :, self.span(k), :], self.sum_sems.at[1], (d, k))
+            total = total + self.line_in[d, :, self.span(k), :].astype(F32)
+        self.back_out[:, self.span(k), :] = total.astype(BF16)
+        for i in self.places(k):
+            if i == 0:
+                self.own_back().start()
+            else:
+                self.back_copy(i).start()
+
+    def own_back(self):
+        return pltpu.make_async_copy(
+            self.back_out.at[:, pl.ds(0, self.cap), :], self.back.at[self.me], self.dp_sems.at[1, 1, 0]
+        )
+
+    def run(self, compute):
+        self.greet()
+        self.send_out()
+        for step in range(self.steps + 4):
+            for lag, work in enumerate((self.spread, self.relay, compute, self.along, self.give)):
+                k = step - lag
+                if 0 <= k < self.steps:
+                    if lag == 2:
+                        self.collect(k)
+                    work(k)
+                    if lag == 2:
+                        self.pair(k)
+
+    def finish(self):
+        self.own_back().wait()
+        for i in range(1, self.groups):
+            where = self.back.at[self.group(i)]
+            self.landed(where, self.dp_sems.at[1], (i,))
+            self.out_copy(i).wait_send()
+            self.back_copy(i).wait_send()
+        for i in range(self.groups):
+            for d in range(self.lines):
+                if d:
+                    self.line_copy(d, i).wait_send()
+                self.mate_copy(d, i).wait_send()
+        for k in range(self.steps):
+            for d in range(self.lines):
+                if d:
+                    self.sum_copy(d, k).wait_send()
+                self.pair_copy(d, k).wait_send()
+
+
+def mover_scratch(groups, shards, local, cap, share, chunk):
+    lines, slots, steps = shards // 2, groups * cap, groups // chunk
+    return [
+        pltpu.VMEM((lines, local, slots, share), BF16),
+        pltpu.VMEM((lines, local, slots, share), BF16),
+        pltpu.VMEM((lines, local, slots, share), BF16),
+        pltpu.VMEM((local, slots, share), BF16),
+        pltpu.SemaphoreType.DMA((2, 2, groups)),
+        pltpu.SemaphoreType.DMA((2, 2, lines, groups)),
+        pltpu.SemaphoreType.DMA((2, 2, lines, steps)),
+    ]
+
+
+ROOT = math.sqrt(2.0 / math.pi)
+
+
+def gelu_parts(v):
+    inner = jnp.tanh(ROOT * (v + 0.044715 * (v * v * v)))
+    half = 0.5 * (1.0 + inner)
+    slope = half + 0.5 * v * (1.0 - inner * inner) * (ROOT * (1.0 + 3.0 * 0.044715 * v * v))
+    return v * half, slope
+
+
+def expert_forward(
+    groups, shards, local, cap, chunk,
+    source, gate_up_hbm, down_hbm,
+    back, rows_hbm, pre_hbm, hidden_hbm,
+    rows, part, gate_up, down, pre, hidden, load_sems, save_sems, *scratch,
+):
+    mover = Mover(groups, shards, cap, chunk, source, rows, part, back, scratch)
+    share = rows.shape[-1]
+    loads = [pltpu.make_async_copy(gate_up_hbm, gate_up, load_sems.at[0]), pltpu.make_async_copy(down_hbm, down, load_sems.at[1])]
+    for load in loads:
+        load.start()
+
+    def saves(k):
+        span = mover.span(k)
+        return [
+            pltpu.make_async_copy(rows.at[:, :, span, :], rows_hbm.at[:, :, span, :], save_sems.at[0, k]),
+            pltpu.make_async_copy(pre.at[:, :, span, :], pre_hbm.at[:, :, span, :], save_sems.at[1, k]),
+            pltpu.make_async_copy(hidden.at[:, span, :], hidden_hbm.at[:, span, :], save_sems.at[2, k]),
+        ]
+
+    def compute(k):
+        span = mover.span(k)
+        if k == 0:
+            for load in loads:
+                load.wait()
+        for e in range(local):
+            lhs = jnp.concatenate([rows[s, e, span, :] for s in range(shards)], axis=1)
+            gate = dot(lhs, gate_up[e, 0])
+            up = dot(lhs, gate_up[e, 1])
+            pre[0, e, span, :] = gate
+            pre[1, e, span, :] = up
+            low = (gelu_parts(gate)[0] * up).astype(BF16)
+            hidden[e, span, :] = low
+            result = dot(low, down[e]).astype(BF16)
+            for s in range(shards):
+                part[s, e, span, :] = result[:, s * share : (s + 1) * share]
+        for save in saves(k):
+            save.start()
+
+    mover.run(compute)
+    mover.finish()
+    for k in range(mover.steps):
+        for save in saves(k):
+            save.wait()
+
+
+def expert_backward(
+    groups, shards, local, cap, chunk,
+    source, gate_up_hbm, down_hbm, pre_hbm,
+    back, rows_hbm, side_hbm,
+    rows, part, gate_up, down, pre, side, load_sems, save_sems, *scratch,
+):
+    mover = Mover(groups, shards, cap, chunk, source, rows, part, back, scratch)
+    share = rows.shape[-1]
+    loads = [
+        pltpu.make_async_copy(gate_up_hbm, gate_up, load_sems.at[0]),
+        pltpu.make_async_copy(down_hbm, down, load_sems.at[1]),
+        pltpu.make_async_copy(pre_hbm, pre, load_sems.at[2]),
+    ]
+    for load in loads:
+        load.start()
+
+    def saves(k):
+        span = mover.span(k)
+        return [
+            pltpu.make_async_copy(rows.at[:, :, span, :], rows_hbm.at[:, :, span, :], save_sems.at[0, k]),
+            pltpu.make_async_copy(side.at[:, :, span, :], side_hbm.at[:, :, span, :], save_sems.at[1, k]),
+        ]
+
+    def compute(k):
+        span = mover.span(k)
+        if k == 0:
+            for load in loads:
+                load.wait()
+        for e in range(local):
+            lhs = jnp.concatenate([rows[s, e, span, :] for s in range(shards)], axis=1)
+            hidden_grad = dot(lhs, down[e], ((1,), (1,)))
+            activated, slope = gelu_parts(pre[0, e, span, :])
+            gate_side = (hidden_grad * pre[1, e, span, :] * slope).astype(BF16)
+            up_side = (hidden_grad * activated).astype(BF16)
+            side[0, e, span, :] = gate_side
+            side[1, e, span, :] = up_side
+            result = dot(gate_side, gate_up[e, 0], ((1,), (1,))) + dot(up_side, gate_up[e, 1], ((1,), (1,)))
+            result = result.astype(BF16)
+            for s in range(shards):
+                part[s, e, span, :] = result[:, s * share : (s + 1) * share]
+        for save in saves(k):
+            save.start()
+
+    mover.run(compute)
+    mover.finish()
+    for k in range(mover.steps):
+        for save in saves(k):
+            save.wait()
+
+
 def rms_scale(values):
     return lax.rsqrt(jnp.mean(values * values, axis=-1, keepdims=True) + EPSILON)
 
@@ -143,10 +437,6 @@
     def gather_columns(values):
         return lax.all_gather(values, "tensor", axis=values.ndim - 1, tiled=True)
 
-    def exchange(values):
-        blocks = values.reshape(groups, slot_count // groups, share)
-        return lax.all_to_all(blocks, "dp", split_axis=0, concat_axis=0, tiled=True)
-
     def scatter_columns(values):
         rows = values.shape[0]
         parts = lax.all_to_all(
@@ -195,17 +485,43 @@
     teacher_mine = mine(teacher).astype(F32)
     normed_mine = mine(normed_two_low)
     dispatched = dot(any_route, normed_mine, ((0,), (0,))).astype(BF16)
-    expert_rows = gather_columns(exchange(dispatched)).reshape(
-        groups, local_experts, padded_cap, model_width
-    )
-    gate_up = jnp.einsum("nxcd,xjdf->jnxcf", expert_rows, w_gate_up, preferred_element_type=F32)
-    activated, gelu_pull = jax.vjp(lambda v: jax.nn.gelu(v, approximate=True), gate_up[0])
-    hidden_low = (activated * gate_up[1]).astype(BF16)
-    partial_out = jnp.einsum(
-        "nxcf,xfd->nxcd", hidden_low, w_down, preferred_element_type=F32
-    ).astype(BF16)
-    summed = scatter_columns(partial_out.reshape(slot_count, model_width)).astype(BF16)
-    returned = exchange(summed).reshape(slot_count, share)
+    chunk = max(groups // 4, 1)
+    slots = groups * padded_cap
+    block_shape = (groups, local_experts, padded_cap, share)
+    rows_type = jax.ShapeDtypeStruct((shards, local_experts, slots, share), BF16)
+    back_type = jax.ShapeDtypeStruct(block_shape, BF16)
+    ff_here = w_down.shape[1]
+    sizes = (groups, shards, local_experts, padded_cap)
+    rows_scratch = [
+        pltpu.VMEM((shards, local_experts, slots, share), BF16),
+        pltpu.VMEM((shards, local_experts, slots, share), BF16),
+        pltpu.VMEM(w_gate_up.shape, BF16),
+        pltpu.VMEM(w_down.shape, BF16),
+        pltpu.VMEM((2, local_experts, slots, ff_here), F32),
+    ]
+    returned, expert_rows, pre_acts, hidden_low = pl.pallas_call(
+        functools.partial(expert_forward, *sizes, chunk),
+        out_shape=(
+            back_type,
+            rows_type,
+            jax.ShapeDtypeStruct((2, local_experts, slots, ff_here), F32),
+            jax.ShapeDtypeStruct((local_experts, slots, ff_here), BF16),
+        ),
+        in_specs=[ANY] * 3,
+        out_specs=(ANY,) * 4,
+        scratch_shapes=rows_scratch
+        + [
+            pltpu.VMEM((local_experts, slots, ff_here), BF16),
+            pltpu.SemaphoreType.DMA((2,)),
+            pltpu.SemaphoreType.DMA((3, groups // chunk)),
+        ]
+        + mover_scratch(*sizes, share, chunk),
+        compiler_params=pltpu.CompilerParams(
+            vmem_limit_bytes=50 * 1024 * 1024, collective_id=1, has_side_effects=True
+        ),
+        name="expert_forward",
+    )(dispatched.reshape(block_shape), w_gate_up, w_down)
+    returned = returned.reshape(slot_count, share)
     routed_first = dot(first_route, returned)
     routed_second = dot(second_route, returned)
 
@@ -227,20 +543,32 @@
         axis=1,
     )
     gate_grad = lax.psum(gate_grad_part, "tensor")
-    expert_grad = gather_columns(exchange(slot_grad)).reshape(
-        groups, local_experts, padded_cap, model_width
-    )
-    down_grad = jnp.einsum("nxcf,nxcd->xfd", hidden_low, expert_grad, preferred_element_type=F32)
-    hidden_grad = jnp.einsum("nxcd,xfd->nxcf", expert_grad, w_down, preferred_element_type=F32)
-    gate_side = gelu_pull(hidden_grad * gate_up[1])[0]
-    up_side = hidden_grad * activated
-    pre_grads = jnp.stack([gate_side, up_side], axis=0).astype(BF16)
-    gate_up_grad = jnp.einsum(
-        "nxcd,jnxcf->xjdf", expert_rows, pre_grads, preferred_element_type=F32
-    )
-    rows_grad = jnp.einsum("jnxcf,xjdf->nxcd", pre_grads, w_gate_up, preferred_element_type=F32)
-    rows_mine = scatter_columns(rows_grad.astype(BF16).reshape(slot_count, model_width))
-    back_grad = exchange(rows_mine.astype(BF16)).reshape(slot_count, share)
+    back_grad, expert_grad, pre_grads = pl.pallas_call(
+        functools.partial(expert_backward, *sizes, chunk),
+        out_shape=(
+            back_type,
+            rows_type,
+            jax.ShapeDtypeStruct((2, local_experts, slots, ff_here), BF16),
+        ),
+        in_specs=[ANY] * 4,
+        out_specs=(ANY,) * 3,
+        scratch_shapes=rows_scratch
+        + [
+            pltpu.VMEM((2, local_experts, slots, ff_here), BF16),
+            pltpu.SemaphoreType.DMA((3,)),
+            pltpu.SemaphoreType.DMA((2, groups // chunk)),
+        ]
+        + mover_scratch(*sizes, share, chunk),
+        compiler_params=pltpu.CompilerParams(
+            vmem_limit_bytes=50 * 1024 * 1024, collective_id=2, has_side_effects=True
+        ),
+        name="expert_backward",
+    )(slot_grad.reshape(block_shape), w_gate_up, w_down, pre_acts)
+    back_grad = back_grad.reshape(slot_count, share)
+    down_grad = jnp.einsum("xmf,sxmc->xfsc", hidden_low, expert_grad, preferred_element_type=F32)
+    down_grad = down_grad.reshape(w_down.shape)
+    gate_up_grad = jnp.einsum("sxmc,jxmf->xjscf", expert_rows, pre_grads, preferred_element_type=F32)
+    gate_up_grad = gate_up_grad.reshape(w_gate_up.shape)
 
     logit_grad = gate_pull(gate_grad)[0].astype(BF16)
     router_grad = dot(normed_two_low, logit_grad, ((0,), (0,)))

time: 552 us -> 387 us (0.70)
  waiting for transfers between devices: 181 us -> 18.1 us
  Pallas kernels: 14.2 us -> 117 us
  blocking collectives: 179 us -> 132 us
  matrix products: 75.6 us -> 43.2 us
  starting transfers between devices: 24 us -> 3.89 us
    pallas_call x0 -> x2, Pallas kernels: none -> 102 us  [the longest x1 52 us: body(): pl.pallas_call(functools.partial(expert_backward, *sizes, chunk), out_sha...]
    all_gather x4 -> x2, waiting for transfers between devices: 64 us -> 0.01 us  [gather_columns(): return lax.all_gather(values, 'tensor', axis=values.ndim - 1, tiled=True)]
    all_to_all x2 -> x0, blocking collectives: 45.7 us -> none  [exchange(): return lax.all_to_all(blocks, 'dp', split_axis=0, concat_axis=0, tiled=True)]
    all_to_all x3 -> x1, waiting for transfers between devices: 40 us -> 0.01 us  [scatter_columns(): lax.all_to_all(values.reshape(rows, shards, share), 'tensor', split_axis=...]
    dot_general x6 -> x2, matrix products: 45.8 us -> 16.8 us  [the longest x1 12 us: body(): jnp.einsum('sxmc,jxmf->xjscf', expert_rows, pre_grads, preferred_element_...]
    all_to_all x2 -> x0, waiting for transfers between devices: 24.6 us -> none  [exchange(): return lax.all_to_all(blocks, 'dp', split_axis=0, concat_axis=0, tiled=True)]
    psum x1, waiting for transfers between devices: 27.2 us -> 9.97 us  [body(): qkv_sum = lax.psum(qkv_grad.astype(BF16), 'dp').astype(F32)]
    all_gather x1, waiting for transfers between devices: 24.2 us -> 7.34 us  [body(): w_out_full = lax.all_gather(w_out, 'tensor', axis=0, tiled=True)]
  transfers between devices with their start and end apart: 11 -> 5, of which waited for: 9 -> 2; matrix products, arithmetic and copies ran while one was open for 6% -> 14% of each run, Pallas kernels for 0% -> 0%
where the time goes in v2:
time: 387 us; the launch traced here: 381 us
  blocking collectives  132 us (34%)
  Pallas kernels  117 us (30%)
  matrix products  43.2 us (11%)
  local copies, waits for them, and re-layouts  32.6 us (8%)
  between operations  18.4 us (5%)
  waiting for transfers between devices  18.1 us (5%)
  other arithmetic  16.3 us (4%)
  starting transfers between devices  3.89 us (1%)
    pallas_call x1, Pallas kernels, body(): pl.pallas_call(functools.partial(expert_backward, *sizes, chunk), out_sha...  52 us
    pallas_call x1, Pallas kernels, body(): pl.pallas_call(functools.partial(expert_forward, *sizes, chunk), out_shap...  50.5 us
    psum x1, blocking collectives, body(): squared = lax.psum(jnp.sum(deviation * deviation), ('dp', 'tensor'))  39.4 us
    psum x1, blocking collectives, body(): router_sum = lax.psum(router_grad.astype(BF16), 'dp').astype(F32)  33.2 us
    psum x1, blocking collectives, body(): valid_total = lax.psum(lengths[0].astype(F32), 'dp')  23.8 us
    psum x1, blocking collectives, body(): table_sum = lax.psum(table_grad, 'dp')  18 us
    unnamed x42, local copies, waits for them, and re-layouts  16.7 us
    dot_general x10, matrix products, dot(): return lax.dot_general(a, b, (dims, ((), ())), preferred_element_type=F32)  15.7 us
  transfers between devices with their start and end apart: 5, of which 2 were waited for; matrix products, arithmetic and copies ran while one was open for 14% of the time, Pallas kernels for 0%

profile of v2, /device:TPU:0, one launch (start us, length us, event | category | flops | bytes accessed | tf_op | source)
XLA Modules:
  0.0 381.2 jit_solution(1229759030934956465)
XLA Ops:
  7.2 0.0 all-gather.4.cloned.1.call-start
  8.0 1.5 multiply_reduce_fusion.1
  9.5 1.1 convolution_bitcast_fusion.1.bias_ref
  10.7 2.3 fusion.14.proj_ref
  12.9 6.6 %attention_forward.1 = (bf16[512,256]{1,0:T(8,128)(2,1)}, f32[4,512,512]{2,1,0:T(8,128)S(1)}) custom-call(s32[1]{0:T(128)} %copy.119.len_ref, f32[4,1024]{1,0:T(4,128)S(1)} %convolution_bitcast_fusion.1.bias_ref, bf16[3,512,256]{2,1,0:T(8,128)(2,1)S(1)} %fusion.14.proj_ref), custom_call_target="tpu_custom_call" | custom-call | tf_op jit(solution)/shard_map/attention_forward/pallas_call | solution.py:456
  19.5 2.0 copy-done.1
  21.6 0.0 all-gather.4.cloned.1.call-update
  21.6 0.0 all-gather.6.cloned.1.call-start
  21.6 0.7 all-gather.6.cloned.1.call-update
  22.3 0.0 all-gather.8.cloned.1.call-start
  22.4 23.8 %psum.71 = f32[]{:T(128)} all-reduce(f32[]{:T(128)S(6)} %convert_element_type.159), channel_id=1, replica_groups=mesh['dp'=8,'tensor'=4] {'dp'}, use_global_device_ids=true, to_apply=%region_8.9 | all-reduce | flops 1 | bytes 8 | tf_op jit(solution)/shard_map/psum | solution.py:529
  46.2 8.5 %copy.74.gate_up_hbm = bf16[2,2,1024,704]{3,2,1,0:T(8,128)(2,1)} copy(bf16[2,2,1024,704]{2,3,1,0:T(8,128)(2,1)} %param.24) | data formatting | bytes 11534336 | tf_op args[11]
  55.5 0.1 dynamic_slice.25
  55.6 2.5 iota_compare_fusion
  58.1 7.3 %all-gather.6.cloned.1.call-done = bf16[1024,1024]{1,0:T(8,128)(2,1)} async-done(((bf16[256,1024]{1,0:T(8,128)(2,1)}), bf16[1024,1024]{1,0:T(8,128)(2,1)}) %all-gather.6.cloned.1.call-update) | async-done | bytes 2097168 | tf_op jit(solution)/shard_map/all_gather | solution.py:468
  65.5 3.3 multiply_reduce_fusion
  68.8 0.2 multiply_convert_fusion
  69.0 0.5 copy-done.15
  69.5 0.4 fusion.48
  70.1 1.2 copy-done.8
  71.3 0.6 convolution_convert_fusion
  71.9 50.5 %expert_forward.1 = (bf16[8,2,80,256]{3,2,1,0:T(8,128)(2,1)S(1)}, bf16[4,2,640,256]{3,2,1,0:T(8,128)(2,1)}, f32[2,2,640,704]{3,2,1,0:T(8,128)}, bf16[2,640,704]{2,1,0:T(8,128)(2,1)S(1)}) custom-call(bf16[8,2,80,256]{3,2,1,0:T(8,128)(2,1)S(1)} %bitcast.95, bf16[2,2,1024,704]{3,2,1,0:T(8,128)(2,1)} %copy.74.gate_up_hbm, bf16[2,704,1024]{2,1,0:T(8,128)(2,1)} %down_hbm.3), custom_call_target="tpu_custom_call" | custom-call | tf_op jit(solution)/shard_map/expert_forward/pallas_call | solution.py:502
  122.4 0.6 fusion.10
  123.0 3.4 multiply_reduce_fusion.7
  126.4 5.7 %psum.72 = f32[512,2]{0,1:T(2,128)S(1)} all-reduce(f32[512,2]{0,1:T(2,128)S(1)} %pad_maximum_fusion.1), channel_id=1, replica_groups=mesh['dp'=8,'tensor'=4] {'tensor'}, use_global_device_ids=true, to_apply=%region_11.12 | all-reduce | flops 1024 | bytes 8192 | tf_op jit(solution)/shard_map/psum | solution.py:545
  132.2 2.4 fusion.8
  134.7 1.0 fusion.4
  135.6 0.4 fusion.49
  136.1 52.0 %expert_backward.1 = (bf16[8,2,80,256]{3,2,1,0:T(8,128)(2,1)S(1)}, bf16[4,2,640,256]{3,2,1,0:T(8,128)(2,1)S(1)}, bf16[2,2,640,704]{3,2,1,0:T(8,128)(2,1)}) custom-call(bf16[8,2,80,256]{3,2,1,0:T(8,128)(2,1)S(1)} %bitcast.94, bf16[2,2,1024,704]{3,2,1,0:T(8,128)(2,1)} %copy.74.gate_up_hbm, bf16[2,704,1024]{2,1,0:T(8,128)(2,1)} %down_hbm.3, ...), custom_call_target="tpu_custom_call" | custom-call | tf_op jit(solution)/shard_map/expert_backward/pallas_call | solution.py:546
  188.1 2.8 multiply_reduce_fusion.2
  190.9 5.6 %psum.73 = f32[512,1]{0,1:T(1,128)S(1)} all-reduce(f32[512,1]{0,1:T(1,128)S(1)} %bitcast.111), channel_id=1, replica_groups=mesh['dp'=8,'tensor'=4] {'tensor'}, use_global_device_ids=true, to_apply=%region_16.17 | all-reduce | flops 512 | bytes 4096 | tf_op jit(solution)/shard_map/psum | solution.py:580
  196.6 2.4 fusion.45
  199.0 0.0 all-gather.8.cloned.1.call-update
  199.0 0.1 dynamic_slice.26
  199.1 2.8 convert_element_type.143
  202.6 0.2 convolution_convert_fusion.5
  202.8 33.2 %psum.79 = bf16[1024,16]{0,1:T(8,128)(2,1)S(1)} all-reduce(bf16[1024,16]{0,1:T(8,128)(2,1)S(1)} %convolution_convert_fusion.5), channel_id=1, replica_groups=mesh['dp'=8,'tensor'=4] {'dp'}, use_global_device_ids=true, to_apply=%region_26.27 | all-reduce | flops 16384 | bytes 65536 | tf_op jit(solution)/shard_map/psum | solution.py:621
  236.0 0.6 convert_element_type.174
  236.6 4.8 %fusion.5 = f32[2,4,88,8,256]{4,3,2,1,0:T(8,128)S(1)} fusion(bf16[4,2,640,256]{3,2,1,0:T(8,128)(2,1)} %copy-done.3, bf16[2,640,704]{2,1,0:T(8,128)(2,1)} %copy-done.4), kind=kOutput, calls=%fused_computation.11 | convolution fusion | flops 1845493760 | bytes 10190848 | tf_op jit(solution)/shard_map/xmf,sxmc->xfsc/dot_general | solution.py:568
  241.5 3.4 copy.103
  244.9 1.7 convolution_convert_fusion.4.grad_ref
  246.6 2.2 copy-done.2
  248.8 7.6 %attention_backward.1 = (bf16[3,512,256]{2,1,0:T(8,128)(2,1)S(1)}, f32[4,1024]{1,0:T(4,128)S(1)}) custom-call(bf16[3,512,256]{2,1,0:T(8,128)(2,1)S(1)} %fusion.14.proj_ref, f32[4,512,512]{2,1,0:T(8,128)S(1)} %copy-done.2, bf16[512,256]{1,0:T(8,128)(2,1)S(1)} %convolution_convert_fusion.4.grad_ref), custom_call_target="tpu_custom_call" | custom-call | tf_op jit(solution)/shard_map/attention_backward/pallas_call | solution.py:590
  256.4 1.0 bitcast_convert_fusion
  257.4 0.2 copy-done.6
  257.6 2.2 fusion.12
  259.9 1.0 copy.113
  260.9 3.5 all-to-all-start
  264.5 0.3 all-reduce.4.cloned.1.call-start
  264.7 2.6 convolution_convert_fusion.3
  267.3 0.0 all-reduce.4.cloned.1.call-update
  267.3 12.0 %convolution_bitcast_fusion = f32[2,2,4,88,8,256]{5,4,3,2,1,0:T(8,128)} fusion(bf16[2,2,640,704]{3,2,1,0:T(8,128)(2,1)} %get-tuple-element.29, bf16[4,2,640,256]{3,2,1,0:T(8,128)(2,1)} %get-tuple-element.30), kind=kOutput, calls=%fused_computation.1 | convolution fusion | flops 3690987520 | bytes 17760256 | tf_op jit(solution)/shard_map/sxmc,jxmf->xjscf/dot_general | solution.py:570
  279.3 10.6 %copy.102 = f32[2,2,4,88,8,256]{5,4,2,3,1,0:T(8,128)} copy(f32[2,2,4,88,8,256]{5,4,3,2,1,0:T(8,128)} %convolution_bitcast_fusion) | data formatting | bytes 23068672 | tf_op jit(solution)/shard_map/reshape | solution.py:571
  289.9 0.4 fusion.18
  290.3 18.0 %psum.78 = f32[32,4]{0,1:T(4,128)} all-reduce(f32[32,4]{0,1:T(4,128)S(1)} %fusion.18), channel_id=1, replica_groups=mesh['dp'=8,'tensor'=4] {'dp'}, use_global_device_ids=true, to_apply=%region_25.26 | all-reduce | flops 128 | bytes 1024 | tf_op jit(solution)/shard_map/psum | solution.py:624
  308.3 0.1 convert_reduce_fusion
  308.5 1.3 multiply_reduce_fusion.3
  309.8 39.4 %all-reduce = (f32[]{:T(128)}, f32[2,1024]{1,0:T(2,128)S(1)}) all-reduce(f32[]{:T(128)} %get-tuple-element.83, f32[2,1024]{1,0:T(2,128)S(1)} %pad_maximum_fusion), channel_id=1, replica_groups=mesh['dp'=8,'tensor'=4] {'dp','tensor'}, use_global_device_ids=true, to_apply=%region_7.8 | all-reduce | flops 2049 | bytes 16392 | tf_op jit(solution)/shard_map/psum | solution.py:534
  349.9 6.3 %psum.74 = f32[512,1]{0,1:T(1,128)S(1)} all-reduce(f32[512,1]{0,1:T(1,128)S(1)} %bitcast.103), channel_id=1, replica_groups=mesh['dp'=8,'tensor'=4] {'tensor'}, use_global_device_ids=true, to_apply=%region_19.20 | all-reduce | flops 512 | bytes 4096 | tf_op jit(solution)/shard_map/psum | solution.py:580
  356.2 0.6 fusion.46
  356.8 2.2 multiply_add_fusion
  359.0 10.0 %all-reduce.4.cloned.1.call-done = (bf16[3,1024,256]{1,2,0:T(8,128)(2,1)}, bf16[256,1024]{1,0:T(8,128)(2,1)}) async-done(((bf16[3,1024,256]{1,2,0:T(8,128)(2,1)}, bf16[256,1024]{1,0:T(8,128)(2,1)}), (bf16[3,1024,256]{1,2,0:T(8,128)(2,1)}, bf16[256,1024]{1,0:T(8,128)(2,1)})) %all-reduce.4.cloned.1.call-update) | async-done | bytes 2097168 | tf_op jit(solution)/shard_map/psum | solution.py:622
  369.0 2.2 convert_element_type.172
  371.2 2.1 copy.88
  (65 shorter events, 0.4 us)
Async XLA Ops:
  7.2 3.5 copy-start
  7.2 50.9 %all-gather.4.cloned.1.call-start = ((), (), s32[]{:S(2)}) async-start(), calls=%async_computation.1 | async-start | bytes 1310720 | tf_op jit(solution)/shard_map/all_gather | solution.py:438
  19.5 2.0 copy-start.1
  21.6 43.9 %all-gather.6.cloned.1.call-start = ((), (), s32[]{:S(2)}) async-start(), calls=%async_computation.2 | async-start | bytes 2621440 | tf_op jit(solution)/shard_map/all_gather | solution.py:468
  22.3 222.6 %all-gather.8.cloned.1.call-start = ((), (), s32[]{:S(2)}) async-start(), calls=%async_computation.3 | async-start | bytes 1310720 | tf_op jit(solution)/shard_map/all_gather | solution.py:438
  46.2 9.3 %copy-start.17 = (f32[1024]{0:T(1024)S(1)}, f32[1024]{0:T(1024)}, u32[]{:S(2)}) copy-start(f32[1024]{0:T(1024)} %param.22) | copy-start | bytes 12292
  46.2 9.4 %copy-start.16 = (s32[512,2]{0,1:T(2,128)S(1)}, s32[512,2]{0,1:T(2,128)}, u32[]{:S(2)}) copy-start(s32[512,2]{0,1:T(2,128)} %param.16) | copy-start | bytes 12292
  46.2 9.4 %copy-start.18 = (s32[512,2]{0,1:T(2,128)S(1)}, s32[512,2]{0,1:T(2,128)}, u32[]{:S(2)}) copy-start(s32[512,2]{0,1:T(2,128)} %param.17) | copy-start | bytes 12292
  54.7 10.7 %copy-start.5 = (bf16[512,1024]{1,0:T(8,128)(2,1)S(1)}, bf16[512,1024]{1,0:T(8,128)(2,1)}, u32[]{:S(2)}) copy-start(bf16[512,1024]{1,0:T(8,128)(2,1)} %param.13) | copy-start | bytes 3145732
  68.7 54.2 %copy-start.7 = (f32[512,1024]{1,0:T(8,128)}, f32[512,1024]{1,0:T(8,128)S(1)}, u32[]{:S(2)}) copy-start(f32[512,1024]{1,0:T(8,128)S(1)} %get-tuple-element.105) | copy-start | bytes 6291460
  68.7 0.8 copy-start.15
  68.8 2.5 copy-start.8
  71.9 50.5 %copy-start.11 = (pred[512,2,1280]{2,0,1:T(32,128)(4,1)S(1)}, pred[512,2,1280]{2,0,1:T(32,128)(4,1)}, u32[]{:S(2)}) copy-start(pred[512,2,1280]{2,0,1:T(32,128)(4,1)} %get-tuple-element.98) | copy-start | bytes 3932164
  122.3 4.0 %copy-start.4 = (bf16[2,640,704]{2,1,0:T(8,128)(2,1)}, bf16[2,640,704]{2,1,0:T(8,128)(2,1)S(1)}, u32[]{:S(2)}) copy-start(bf16[2,640,704]{2,1,0:T(8,128)(2,1)S(1)} %get-tuple-element.31) | copy-start | bytes 5406724
  132.1 2.6 copy-start.12
  132.1 2.6 copy-start.14
  136.1 52.0 %copy-start.9 = (bf16[512,2,1280]{2,0,1:T(8,128)(2,1)S(1)}, bf16[512,2,1280]{2,0,1:T(8,128)(2,1)}, u32[]{:S(2)}) copy-start(bf16[512,2,1280]{2,0,1:T(8,128)(2,1)} %get-tuple-element.99) | copy-start | bytes 7864324
  188.1 2.8 copy-start.3
  190.9 8.1 %copy-start.19 = (f32[1024]{0:T(1024)S(1)}, f32[1024]{0:T(1024)}, u32[]{:S(2)}) copy-start(f32[1024]{0:T(1024)} %param.18) | copy-start | bytes 12292
  241.5 3.4 copy-start.13
  246.6 2.2 copy-start.2
  256.4 1.2 copy-start.6
  260.9 47.4 %all-to-all-start = ((bf16[512,4,256]{2,0,1:T(8,128)(2,1)}), bf16[512,4,256]{2,0,1:T(8,128)(2,1)S(1)}, u32[]{:S(2)}, u32[]{:S(2)}) async-start(bf16[512,4,256]{2,0,1:T(8,128)(2,1)} %bitcast.101), calls=%async_computation | async-start | bytes 2097152 | tf_op jit(solution)/shard_map/all_to_all | solution.py:442
  264.5 104.5 %all-reduce.4.cloned.1.call-start = ((), (), s32[]{:S(2)}) async-start(), calls=%async_computation.4 | async-start | bytes 4194304 | tf_op jit(solution)/shard_map/psum | solution.py:622
  369.0 2.2 copy-start.10
Sparse Core Ops, SparseCore 0:
  21.7 19.5 all-gather.3
  42.8 22.5 all-gather.5
  199.1 13.7 all-gather.7
  268.6 100.2 all-reduce.3

commit v3 on v2

--- a/solution.py
+++ b/solution.py
@@ -63,40 +63,6 @@
             probs = exponent * (1.0 / jnp.sum(exponent, axis=1, keepdims=True))
             probs_ref[h, rows, :] = probs
             attended_ref[rows, cols] = dot(probs.astype(BF16), values).astype(BF16)
-
-
-def attention_backward(heads, width, proj_ref, probs_ref, grad_ref, out_ref, diag_ref, acc, key_acc, value_acc):
-    for h in range(heads):
-        cols = slice(h * width, (h + 1) * width)
-        keys = proj_ref[1, :, cols]
-        values = proj_ref[2, :, cols]
-        acc[...] = jnp.zeros_like(acc)
-        for j in range(SEQ_LEN // TILE):
-            rows = slice(j * TILE, (j + 1) * TILE)
-            start = SEQ_LEN - j * TILE
-            probs = probs_ref[h, rows, :]
-            grad = grad_ref[rows, cols]
-            prob_grad = dot(grad, values, ((1,), (1,)))
-            score_grad = probs * (prob_grad - jnp.sum(probs * prob_grad, axis=1, keepdims=True))
-            acc[:, start : start + SEQ_LEN] += score_grad
-            low = score_grad.astype(BF16)
-            out_ref[0, rows, cols] = dot(low, keys).astype(BF16)
-            key_part = dot(low, proj_ref[0, rows, cols], ((0,), (0,)))
-            value_part = dot(probs.astype(BF16), grad, ((0,), (0,)))
-            if j == 0:
-                key_acc[...] = key_part
-                value_acc[...] = value_part
-            else:
-                key_acc[...] += key_part
-                value_acc[...] += value_part
-        out_ref[1, :, cols] = key_acc[...].astype(BF16)
-        out_ref[2, :, cols] = value_acc[...].astype(BF16)
-        total = acc[...]
-        half = TILE // 2
-        while half >= 1:
-            total = total[:half] + pltpu.roll(total[half : 2 * half], SPAN - half, 1)
-            half //= 2
-        diag_ref[h : h + 1, :] = total
 
 
 VMEM = pl.BlockSpec(memory_space=pltpu.VMEM)
@@ -247,7 +213,6 @@
         )
 
     def run(self, compute):
-        self.greet()
         self.send_out()
         for step in range(self.steps + 4):
             for lag, work in enumerate((self.spread, self.relay, compute, self.along, self.give)):
@@ -303,9 +268,9 @@
 
 def expert_forward(
     groups, shards, local, cap, chunk,
-    source, gate_up_hbm, down_hbm,
-    back, rows_hbm, pre_hbm, hidden_hbm,
-    rows, part, gate_up, down, pre, hidden, load_sems, save_sems, *scratch,
+    source, gate_up_hbm, down_hbm, count,
+    back, rows_hbm, pre_hbm, hidden_hbm, total,
+    rows, part, gate_up, down, pre, hidden, load_sems, save_sems, counts, count_sems, *scratch,
 ):
     mover = Mover(groups, shards, cap, chunk, source, rows, part, back, scratch)
     share = rows.shape[-1]
@@ -328,8 +293,8 @@
                 load.wait()
         for e in range(local):
             lhs = jnp.concatenate([rows[s, e, span, :] for s in range(shards)], axis=1)
-            gate = dot(lhs, gate_up[e, 0])
-            up = dot(lhs, gate_up[e, 1])
+            gate = dot(lhs, gate_up[e, 0], ((1,), (1,)))
+            up = dot(lhs, gate_up[e, 1], ((1,), (1,)))
             pre[0, e, span, :] = gate
             pre[1, e, span, :] = up
             low = (gelu_parts(gate)[0] * up).astype(BF16)
@@ -340,7 +305,18 @@
         for save in saves(k):
             save.start()
 
+    def count_copy(i):
+        return mover.remote(count, counts.at[i], count_sems, (i,), {"dp": mover.group(i)})
+
+    mover.greet()
+    for i in range(1, groups):
+        count_copy(i).start()
     mover.run(compute)
+    tally = count[...]
+    for i in range(1, groups):
+        count_copy(i).wait()
+        tally = tally + counts[i]
+    total[...] = tally
     mover.finish()
     for k in range(mover.steps):
         for save in saves(k):
@@ -383,18 +359,375 @@
             up_side = (hidden_grad * activated).astype(BF16)
             side[0, e, span, :] = gate_side
             side[1, e, span, :] = up_side
-            result = dot(gate_side, gate_up[e, 0], ((1,), (1,))) + dot(up_side, gate_up[e, 1], ((1,), (1,)))
+            result = dot(gate_side, gate_up[e, 0]) + dot(up_side, gate_up[e, 1])
             result = result.astype(BF16)
             for s in range(shards):
                 part[s, e, span, :] = result[:, s * share : (s + 1) * share]
         for save in saves(k):
             save.start()
 
+    mover.greet()
     mover.run(compute)
     mover.finish()
     for k in range(mover.steps):
         for save in saves(k):
             save.wait()
+
+
+def weight_grads(shards, rows, grads, side, hidden, gate_up_out, down_out):
+    step = pl.program_id(1)
+    share = rows.shape[-1]
+
+    @pl.when(step < 2)
+    def _():
+        for s in range(shards):
+            gate_up_out[:, s * share : (s + 1) * share] = dot(side[...], rows[s], ((0,), (0,)))
+
+    @pl.when(step == 2)
+    def _():
+        for s in range(shards):
+            down_out[:, s * share : (s + 1) * share] = dot(hidden[...], grads[s], ((0,), (0,)))
+
+
+def to_row(column):
+    rows = column.shape[0]
+    return jnp.transpose(jnp.broadcast_to(column, (rows, 128)))[:8]
+
+
+def to_column(row):
+    return jnp.transpose(jnp.broadcast_to(row[:1], (128, row.shape[1])))[:, :1]
+
+
+def dense_backward(
+    groups, shards, heads, width, experts,
+    norm_grad, after, out_grad, residual, scales, gains, extras_in, onehot,
+    attended_hbm, w_out_hbm, proj_hbm, probs_hbm, normed_hbm, w_qkv_hbm,
+    dense_out, input_grad, extras_out,
+    attended, w_out, proj, probs, normed, w_qkv, load_sems,
+    dots, dot_sems, branch, branch_sems, grad_here, diag, key_acc, value_acc, proj_grad,
+    part, mate_in, line_out, line_in, part_sems,
+    dense, result, y_in, y_sum, z_in, dense_sems, z_sems, save_sems,
+    extras, extras_in_dp, extras_sems, extras_ring_sems,
+):
+    model = normed.shape[1]
+    share = branch.shape[-1]
+    tokens = branch.shape[1]
+    here = heads * width
+    lines = shards // 2
+    y_size = 1 << ((groups.bit_length() - 1) // 2)
+    z_size = groups // y_size
+    pieces = dense.shape[0]
+    me, place = lax.axis_index("dp"), lax.axis_index("tensor")
+    line, core = lax.div(place, 2), lax.rem(place, 2)
+    z, y = lax.div(me, y_size), lax.rem(me, y_size)
+    mate = {"tensor": line * 2 + 1 - core}
+    inverse = 1.0 / model
+
+    def group(i):
+        return lax.rem(me + i, groups)
+
+    def shard(d, c):
+        return lax.rem(line + d, lines) * 2 + c
+
+    def near(i):
+        return lax.rem(place + i, shards)
+
+    def remote(src, dst, sems, index, device):
+        return pltpu.make_async_remote_copy(
+            src_ref=src, dst_ref=dst, send_sem=sems.at[(0, *index)], recv_sem=sems.at[(1, *index)],
+            device_id=device, device_id_type=MESH_ID,
+        )
+
+    def landed(where, sems, index):
+        remote(where, where, sems, index, mate).wait_recv()
+
+    loads = [
+        pltpu.make_async_copy(src, dst, load_sems.at[n])
+        for n, (src, dst) in enumerate(
+            (
+                (w_out_hbm, w_out), (attended_hbm, attended), (proj_hbm, proj), (probs_hbm, probs),
+                (w_qkv_hbm, w_qkv), (normed_hbm, normed),
+            )
+        )
+    ]
+    for load in loads:
+        load.start()
+
+    barrier = pltpu.get_barrier_semaphore()
+    for i in range(1, groups):
+        pl.semaphore_signal(barrier, inc=1, device_id={"dp": group(i)}, device_id_type=MESH_ID)
+    for i in range(1, shards):
+        pl.semaphore_signal(barrier, inc=1, device_id={"tensor": near(i)}, device_id_type=MESH_ID)
+    pl.semaphore_wait(barrier, groups + shards - 2)
+
+    def dot_copy(n, i):
+        return remote(dots.at[n, 0], dots.at[n, i], dot_sems, (n, i), {"tensor": near(i)})
+
+    def dot_send(n, column):
+        dots[n, 0] = to_row(column)
+        for i in range(1, shards):
+            dot_copy(n, i).start()
+
+    def dot_sum(n):
+        total = dots[n, 0]
+        for i in range(1, shards):
+            dot_copy(n, i).wait()
+            total = total + dots[n, i]
+        return to_column(total)
+
+    scale_two = scales[:, 1:2]
+    weighted = norm_grad[...] * gains[1:2, :]
+    dot_send(0, jnp.sum(weighted * after[...], axis=1, keepdims=True))
+    extras[0] = extras_in[...]
+    extras[0, experts + 1 : experts + 2, :] = jnp.sum(norm_grad[...] * after[...] * scale_two, axis=0, keepdims=True)
+    along = dot_sum(0)
+    after_grad = out_grad[...] + scale_two * (weighted - after[...] * (scale_two * scale_two * along * inverse))
+    grad_here[...] = after_grad
+    branch[place] = after_grad.astype(BF16)
+
+    blocks = tokens // TILE
+
+    def row_block(j):
+        return pl.ds(j * TILE, TILE)
+
+    def branch_line(d, j):
+        where = branch.at[place, row_block(j), :]
+        return remote(where, where, branch_sems.at[0], (d, j), {"tensor": shard(d, core)})
+
+    def branch_mate(d, j):
+        where = branch.at[shard(lines - d, core), row_block(j), :]
+        return remote(where, where, branch_sems.at[1], (d, j), mate)
+
+    for j in range(blocks):
+        for d in range(1, lines):
+            branch_line(d, j).start()
+        branch_mate(0, j).start()
+    for j in range(blocks):
+        for d in range(1, lines):
+            landed(branch.at[shard(lines - d, core), row_block(j), :], branch_sems.at[0], (d, j))
+            branch_mate(d, j).start()
+    for j in range(blocks):
+        for d in range(lines):
+            landed(branch.at[shard(lines - d, 1 - core), row_block(j), :], branch_sems.at[1], (d, j))
+    loads[0].wait()
+    loads[1].wait()
+
+    y_rows, z_rows = model // y_size, model // groups
+
+    def y_copy(p, a):
+        to = lax.rem(y + a, y_size)
+        return remote(
+            dense.at[p, pl.ds(to * y_rows, y_rows), :], y_in.at[p, a], dense_sems.at[0], (p, a), {"dp": z * y_size + to}
+        )
+
+    def z_copy(p, b):
+        to = lax.rem(z + b, z_size)
+        return remote(
+            y_sum.at[p, pl.ds(to * z_rows, z_rows), :], z_in.at[p, b], z_sems.at[0], (p, b), {"dp": to * y_size + y}
+        )
+
+    def z_spread(p, b):
+        to = lax.rem(z + b, z_size)
+        where = result.at[p, pl.ds(y * y_rows + z * z_rows, z_rows), :]
+        return remote(where, where, z_sems.at[1], (p, b), {"dp": to * y_size + y})
+
+    def y_spread(p, a):
+        to = lax.rem(y + a, y_size)
+        where = result.at[p, pl.ds(y * y_rows, y_rows), :]
+        return remote(where, where, dense_sems.at[1], (p, a), {"dp": z * y_size + to})
+
+    def reduce_start(p):
+        for a in range(1, y_size):
+            y_copy(p, a).start()
+
+    def reduce_y(p):
+        total = dense[p, pl.ds(y * y_rows, y_rows), :].astype(F32)
+        for a in range(1, y_size):
+            landed(y_in.at[p, a], dense_sems.at[0], (p, a))
+            total = total + y_in[p, a].astype(F32)
+        y_sum[p] = total.astype(BF16)
+        for b in range(1, z_size):
+            z_copy(p, b).start()
+
+    def reduce_z(p):
+        total = y_sum[p, pl.ds(z * z_rows, z_rows), :].astype(F32)
+        for a in range(1, y_size):
+            y_copy(p, a).wait_send()
+        for b in range(1, z_size):
+            landed(z_in.at[p, b], z_sems.at[0], (p, b))
+            total = total + z_in[p, b].astype(F32)
+        result[p, pl.ds(y * y_rows + z * z_rows, z_rows), :] = total.astype(BF16)
+        for b in range(1, z_size):
+            z_spread(p, b).start()
+
+    def spread_z(p):
+        for b in range(1, z_size):
+            origin = lax.rem(z + z_size - b, z_size)
+            landed(result.at[p, pl.ds(y * y_rows + origin * z_rows, z_rows), :], z_sems.at[1], (p, b))
+        for a in range(1, y_size):
+            y_spread(p, a).start()
+
+    def save(p):
+        return pltpu.make_async_copy(result.at[p], dense_out.at[p], save_sems.at[p])
+
+    def spread_y(p):
+        for a in range(1, y_size):
+            origin = lax.rem(y + y_size - a, y_size)
+            landed(result.at[p, pl.ds(origin * y_rows, y_rows), :], dense_sems.at[1], (p, a))
+        save(p).start()
+
+    for s in range(shards):
+        dense[0, s * here : (s + 1) * here, :] = dot(
+            attended[...], branch[s], ((0,), (0,))
+        ).astype(BF16)
+    reduce_start(0)
+
+    loads[2].wait()
+    loads[3].wait()
+    diag[...] = jnp.zeros_like(diag)
+    for j in range(blocks):
+        rows = slice(j * TILE, (j + 1) * TILE)
+        start = SEQ_LEN - j * TILE
+        wide = jnp.concatenate([branch[s, rows, :] for s in range(shards)], axis=1)
+        grads = dot(wide, w_out[...], ((1,), (1,))).astype(BF16)
+        for h in range(heads):
+            cols = slice(h * width, (h + 1) * width)
+            p = probs[h, rows, :]
+            grad = grads[:, cols]
+            prob_grad = dot(grad, proj[2, :, cols], ((1,), (1,)))
+            score_grad = p * (prob_grad - jnp.sum(p * prob_grad, axis=1, keepdims=True))
+            diag[h, :, start : start + SEQ_LEN] += score_grad
+            low = score_grad.astype(BF16)
+            proj_grad[0, rows, cols] = dot(low, proj[1, :, cols]).astype(BF16)
+            key_part = dot(low, proj[0, rows, cols], ((0,), (0,)))
+            value_part = dot(p.astype(BF16), grad, ((0,), (0,)))
+            if j == 0:
+                key_acc[:, cols] = key_part
+                value_acc[:, cols] = value_part
+            else:
+                key_acc[:, cols] += key_part
+                value_acc[:, cols] += value_part
+        if j == 1:
+            reduce_y(0)
+    proj_grad[1] = key_acc[...].astype(BF16)
+    proj_grad[2] = value_acc[...].astype(BF16)
+    reduce_z(0)
+
+    loads[4].wait()
+    loads[5].wait()
+    for p in range(1, pieces):
+        dense[p] = dot(normed[...], proj_grad[p - 1], ((0,), (0,))).astype(BF16)
+        reduce_start(p)
+    half = tokens // 2
+
+    def part_rows(k):
+        return pl.ds(k * half, half)
+
+    def pair_copy(d, k):
+        return remote(
+            part.at[shard(d, 1 - core), part_rows(k), :], mate_in.at[d, part_rows(k), :], part_sems.at[0], (d, k), mate
+        )
+
+    def line_copy(d, k):
+        return remote(
+            line_out.at[d, part_rows(k), :], line_in.at[d, part_rows(k), :], part_sems.at[1], (d, k),
+            {"tensor": shard(d, core)},
+        )
+
+    for k in range(2):
+        rows = slice(k * half, (k + 1) * half)
+        total = dot(proj_grad[0, rows, :], w_qkv[0], ((1,), (1,)))
+        for n in range(1, 3):
+            total = total + dot(proj_grad[n, rows, :], w_qkv[n], ((1,), (1,)))
+        low = total.astype(BF16)
+        for s in range(shards):
+            part[s, rows, :] = low[:, s * share : (s + 1) * share]
+        for d in range(lines):
+            pair_copy(d, k).start()
+    spread_z(0)
+
+    def pair_sum(d, rows):
+        return part[shard(d, core), rows, :].astype(F32) + mate_in[d, rows, :].astype(F32)
+
+    for k in range(2):
+        rows = part_rows(k)
+        for d in range(lines):
+            landed(mate_in.at[d, rows, :], part_sems.at[0], (d, k))
+        for d in range(1, lines):
+            line_out[d, rows, :] = pair_sum(d, rows).astype(BF16)
+            line_copy(d, k).start()
+    for h in range(heads):
+        total = diag[h]
+        size = TILE // 2
+        while size >= 1:
+            total = total[:size] + pltpu.roll(total[size : 2 * size], SPAN - size, 1)
+            size //= 2
+        row = jnp.broadcast_to(total, (8, SPAN))
+        high = row.astype(BF16)
+        middle = (row - high.astype(F32)).astype(BF16)
+        low = (row - high.astype(F32) - middle.astype(F32)).astype(BF16)
+        table = dot(high, onehot[...]) + dot(middle, onehot[...]) + dot(low, onehot[...])
+        extras[0, experts + 4 + h : experts + 5 + h, : onehot.shape[1]] = table[:1]
+    for p in range(1, pieces):
+        reduce_y(p)
+
+    total = pair_sum(0, pl.ds(0, tokens))
+    for k in range(2):
+        for d in range(1, lines):
+            landed(line_in.at[d, part_rows(k), :], part_sems.at[1], (d, k))
+    for d in range(1, lines):
+        total = total + line_in[d].astype(F32)
+    scale_one = scales[:, 0:1]
+    values = residual[...].astype(F32)
+    weighted = total * gains[0:1, :]
+    dot_send(1, jnp.sum(weighted * values, axis=1, keepdims=True))
+    extras[0, experts : experts + 1, :] = jnp.sum(total * values * scale_one, axis=0, keepdims=True)
+
+    def extras_copy(i):
+        return remote(extras.at[0], extras_in_dp.at[i], extras_sems, (i,), {"dp": group(i)})
+
+    for i in range(1, groups):
+        extras_copy(i).start()
+    for p in range(1, pieces):
+        reduce_z(p)
+    along = dot_sum(1)
+    input_grad[...] = grad_here[...] + scale_one * (weighted - values * (scale_one * scale_one * along * inverse))
+
+    summed = extras[0]
+    for i in range(1, groups):
+        extras_copy(i).wait()
+        summed = summed + extras_in_dp[i]
+    extras_out[place] = summed
+
+    def ring_copy(i):
+        return remote(extras_out.at[place], extras_out.at[place], extras_ring_sems, (i,), {"tensor": near(i)})
+
+    for i in range(1, shards):
+        ring_copy(i).start()
+    for p in range(1, pieces):
+        spread_z(p)
+    for p in range(pieces):
+        spread_y(p)
+    for i in range(1, shards):
+        landed(extras_out.at[near(shards - i)], extras_ring_sems, (i,))
+        ring_copy(i).wait_send()
+    for j in range(blocks):
+        for d in range(lines):
+            if d:
+                branch_line(d, j).wait_send()
+            branch_mate(d, j).wait_send()
+    for k in range(2):
+        for d in range(lines):
+            if d:
+                line_copy(d, k).wait_send()
+            pair_copy(d, k).wait_send()
+    for p in range(pieces):
+        for b in range(1, z_size):
+            z_copy(p, b).wait_send()
+            z_spread(p, b).wait_send()
+        for a in range(1, y_size):
+            y_spread(p, a).wait_send()
+        save(p).wait()
 
 
 def rms_scale(values):
@@ -437,13 +770,6 @@
     def gather_columns(values):
         return lax.all_gather(values, "tensor", axis=values.ndim - 1, tiled=True)
 
-    def scatter_columns(values):
-        rows = values.shape[0]
-        parts = lax.all_to_all(
-            values.reshape(rows, shards, share), "tensor", split_axis=1, concat_axis=1, tiled=True
-        )
-        return jnp.sum(parts.astype(F32), axis=1)
-
     offsets = jnp.arange(SPAN, dtype=jnp.int32) - SEQ_LEN
     onehot_offsets = bucket_onehot(offsets)
     offset_bias = jnp.dot(onehot_offsets, rel_table, precision=highest).T
@@ -485,6 +811,7 @@
     teacher_mine = mine(teacher).astype(F32)
     normed_mine = mine(normed_two_low)
     dispatched = dot(any_route, normed_mine, ((0,), (0,))).astype(BF16)
+    gate_up_t = jnp.swapaxes(w_gate_up, 2, 3)
     chunk = max(groups // 4, 1)
     slots = groups * padded_cap
     block_shape = (groups, local_experts, padded_cap, share)
@@ -495,45 +822,45 @@
     rows_scratch = [
         pltpu.VMEM((shards, local_experts, slots, share), BF16),
         pltpu.VMEM((shards, local_experts, slots, share), BF16),
-        pltpu.VMEM(w_gate_up.shape, BF16),
+        pltpu.VMEM(gate_up_t.shape, BF16),
         pltpu.VMEM(w_down.shape, BF16),
         pltpu.VMEM((2, local_experts, slots, ff_here), F32),
     ]
-    returned, expert_rows, pre_acts, hidden_low = pl.pallas_call(
+    returned, expert_rows, pre_acts, hidden_low, count_total = pl.pallas_call(
         functools.partial(expert_forward, *sizes, chunk),
         out_shape=(
             back_type,
             rows_type,
             jax.ShapeDtypeStruct((2, local_experts, slots, ff_here), F32),
             jax.ShapeDtypeStruct((local_experts, slots, ff_here), BF16),
+            jax.ShapeDtypeStruct((8, 128), jnp.int32),
         ),
-        in_specs=[ANY] * 3,
-        out_specs=(ANY,) * 4,
+        in_specs=[ANY] * 3 + [VMEM],
+        out_specs=(ANY,) * 4 + (VMEM,),
         scratch_shapes=rows_scratch
         + [
             pltpu.VMEM((local_experts, slots, ff_here), BF16),
             pltpu.SemaphoreType.DMA((2,)),
             pltpu.SemaphoreType.DMA((3, groups // chunk)),
+            pltpu.VMEM((groups, 8, 128), jnp.int32),
+            pltpu.SemaphoreType.DMA((2, groups)),
         ]
         + mover_scratch(*sizes, share, chunk),
         compiler_params=pltpu.CompilerParams(
             vmem_limit_bytes=50 * 1024 * 1024, collective_id=1, has_side_effects=True
         ),
         name="expert_forward",
-    )(dispatched.reshape(block_shape), w_gate_up, w_down)
+    )(dispatched.reshape(block_shape), gate_up_t, w_down, jnp.broadcast_to(lengths, (8, 128)))
     returned = returned.reshape(slot_count, share)
     routed_first = dot(first_route, returned)
     routed_second = dot(second_route, returned)
 
     row_alive = (jnp.arange(tok_rows, dtype=jnp.int32) < lengths[0]).astype(F32)[:, None]
-    valid_total = lax.psum(lengths[0].astype(F32), "dp")
+    valid_total = count_total[0, 0].astype(F32)
     scale = groups * tok_rows / valid_total
     block_out = after_mine + gates[:, 0, None] * routed_first + gates[:, 1, None] * routed_second
     deviation = (block_out - teacher_mine) * row_alive
     out_grad = deviation * scale
-    squared = lax.psum(jnp.sum(deviation * deviation), ("dp", "tensor"))
-    loss = squared / (2.0 * valid_total * model_width)
-
     slot_grad = (
         dot(first_route, (gates[:, 0, None] * out_grad).astype(BF16), ((0,), (0,)))
         + dot(second_route, (gates[:, 1, None] * out_grad).astype(BF16), ((0,), (0,)))
@@ -563,75 +890,122 @@
             vmem_limit_bytes=50 * 1024 * 1024, collective_id=2, has_side_effects=True
         ),
         name="expert_backward",
-    )(slot_grad.reshape(block_shape), w_gate_up, w_down, pre_acts)
+    )(slot_grad.reshape(block_shape), gate_up_t, w_down, pre_acts)
     back_grad = back_grad.reshape(slot_count, share)
-    down_grad = jnp.einsum("xmf,sxmc->xfsc", hidden_low, expert_grad, preferred_element_type=F32)
-    down_grad = down_grad.reshape(w_down.shape)
-    gate_up_grad = jnp.einsum("sxmc,jxmf->xjscf", expert_rows, pre_grads, preferred_element_type=F32)
-    gate_up_grad = gate_up_grad.reshape(w_gate_up.shape)
+    gate_up_grad, down_grad = pl.pallas_call(
+        functools.partial(weight_grads, shards),
+        grid=(local_experts, 3),
+        out_shape=(
+            jax.ShapeDtypeStruct(gate_up_t.shape, F32),
+            jax.ShapeDtypeStruct(w_down.shape, F32),
+        ),
+        in_specs=[
+            pl.BlockSpec((shards, None, slots, share), lambda e, j: (0, e, 0, 0)),
+            pl.BlockSpec((shards, None, slots, share), lambda e, j: (0, e, 0, 0)),
+            pl.BlockSpec((None, None, slots, ff_here), lambda e, j: (jnp.minimum(j, 1), e, 0, 0)),
+            pl.BlockSpec((None, slots, ff_here), lambda e, j: (e, 0, 0)),
+        ],
+        out_specs=(
+            pl.BlockSpec((None, None, ff_here, model_width), lambda e, j: (e, jnp.minimum(j, 1), 0, 0)),
+            pl.BlockSpec((None, ff_here, model_width), lambda e, j: (e, 0, 0)),
+        ),
+        compiler_params=pltpu.CompilerParams(vmem_limit_bytes=48 * 1024 * 1024),
+        name="weight_grads",
+    )(expert_rows, expert_grad, pre_grads, hidden_low)
+    gate_up_grad = jnp.swapaxes(gate_up_grad, 2, 3)
 
     logit_grad = gate_pull(gate_grad)[0].astype(BF16)
-    router_grad = dot(normed_two_low, logit_grad, ((0,), (0,)))
+    router_mine = dot(logit_grad, normed_mine, ((0,), (0,)))
     normed_two_grad = dot(any_route, back_grad) + mine(dot(logit_grad, w_router, ((1,), (1,))))
-    gain_two_mine = mine(gain_moe)
-
-    def rms_back(values, factor, gain, grad):
-        projected_part = jnp.sum(grad * gain * values, axis=-1, keepdims=True)
-        along = lax.psum(projected_part, "tensor")
-        gain_grad = jnp.sum(grad * values * factor, axis=0)
-        return factor * (grad * gain - values * (factor * factor * along / model_width)), gain_grad
-
-    after_norm_grad, gain_moe_mine = rms_back(after_mine, scale_two, gain_two_mine, normed_two_grad)
-    after_grad = out_grad + after_norm_grad
-    branch_grad = gather_columns(after_grad.astype(BF16))
-    out_proj_grad = dot(attended, branch_grad, ((0,), (0,)))
-    attended_grad = dot(branch_grad, w_out, ((1,), (1,))).astype(BF16)
-
-    projected_grad, diagonals = pl.pallas_call(
-        functools.partial(attention_backward, heads_here, head_width),
+    squared = jnp.sum(deviation * deviation)
+    extra_rows = experts + 8
+    extras = jnp.concatenate(
+        [router_mine, jnp.zeros((2, share), F32), jnp.broadcast_to(squared, (1, share)), jnp.zeros((5, share), F32)]
+    )
+    y_size = 1 << ((groups.bit_length() - 1) // 2)
+    z_size = groups // y_size
+    lines = shards // 2
+    blocks = tok_rows // TILE
+    pieces = 1 + 3
+    dense, input_grad, extras = pl.pallas_call(
+        functools.partial(dense_backward, groups, shards, heads_here, head_width, experts),
         out_shape=(
-            jax.ShapeDtypeStruct((3, tok_rows, width_here), BF16),
-            jax.ShapeDtypeStruct((heads_here, SPAN), F32),
+            jax.ShapeDtypeStruct((pieces, model_width, width_here), BF16),
+            jax.ShapeDtypeStruct((tok_rows, share), F32),
+            jax.ShapeDtypeStruct((shards, extra_rows, share), F32),
         ),
-        in_specs=[VMEM, VMEM, VMEM],
-        out_specs=(VMEM, VMEM),
+        in_specs=[VMEM] * 8 + [ANY] * 6,
+        out_specs=(ANY, VMEM, VMEM),
         scratch_shapes=[
-            pltpu.VMEM((TILE, SPAN), F32),
-            pltpu.VMEM((SEQ_LEN, head_width), F32),
-            pltpu.VMEM((SEQ_LEN, head_width), F32),
+            pltpu.VMEM(attended.shape, BF16),
+            pltpu.VMEM(w_out.shape, BF16),
+            pltpu.VMEM(projected.shape, BF16),
+            pltpu.VMEM(probs.shape, F32),
+            pltpu.VMEM(normed_low.shape, BF16),
+            pltpu.VMEM(w_qkv.shape, BF16),
+            pltpu.SemaphoreType.DMA((6,)),
+            pltpu.VMEM((2, shards, 8, tok_rows), F32),
+            pltpu.SemaphoreType.DMA((2, 2, shards)),
+            pltpu.VMEM((shards, tok_rows, share), BF16),
+            pltpu.SemaphoreType.DMA((2, 2, lines, blocks)),
+            pltpu.VMEM((tok_rows, share), F32),
+            pltpu.VMEM((heads_here, TILE, SPAN), F32),
+            pltpu.VMEM((SEQ_LEN, width_here), F32),
+            pltpu.VMEM((SEQ_LEN, width_here), F32),
+            pltpu.VMEM((3, tok_rows, width_here), BF16),
+            pltpu.VMEM((shards, tok_rows, share), BF16),
+            pltpu.VMEM((lines, tok_rows, share), BF16),
+            pltpu.VMEM((lines, tok_rows, share), BF16),
+            pltpu.VMEM((lines, tok_rows, share), BF16),
+            pltpu.SemaphoreType.DMA((2, 2, lines, 2)),
+            pltpu.VMEM((pieces, model_width, width_here), BF16),
+            pltpu.VMEM((pieces, model_width, width_here), BF16),
+            pltpu.VMEM((pieces, y_size, model_width // y_size, width_here), BF16),
+            pltpu.VMEM((pieces, model_width // y_size, width_here), BF16),
+            pltpu.VMEM((pieces, z_size, model_width // groups, width_here), BF16),
+            pltpu.SemaphoreType.DMA((2, 2, pieces, y_size)),
+            pltpu.SemaphoreType.DMA((2, 2, pieces, z_size)),
+            pltpu.SemaphoreType.DMA((pieces,)),
+            pltpu.VMEM((1, extra_rows, share), F32),
+            pltpu.VMEM((groups, extra_rows, share), F32),
+            pltpu.SemaphoreType.DMA((2, groups)),
+            pltpu.SemaphoreType.DMA((2, shards)),
         ],
-        compiler_params=pltpu.CompilerParams(vmem_limit_bytes=32 * 1024 * 1024),
-        name="attention_backward",
-    )(projected, probs, attended_grad)
-    table_grad = jnp.dot(onehot_offsets.T, diagonals.T, precision=highest)
-
-    qkv_grad = jnp.einsum("td,jte->jde", normed_low, projected_grad, preferred_element_type=F32)
-    normed_one_part = jnp.einsum("jte,jde->td", projected_grad, w_qkv, preferred_element_type=F32)
-    normed_one_grad = scatter_columns(normed_one_part.astype(BF16))
-    input_norm_grad, gain_attn_mine = rms_back(
-        mine(residual), scale_one, mine(gain_attn), normed_one_grad
+        compiler_params=pltpu.CompilerParams(
+            vmem_limit_bytes=50 * 1024 * 1024, collective_id=3, has_side_effects=True
+        ),
+        name="dense_backward",
+    )(
+        normed_two_grad,
+        after_mine,
+        out_grad,
+        mine(inputs),
+        jnp.concatenate([scale_one, scale_two], axis=1),
+        mine(jnp.stack([gain_attn, gain_moe])),
+        extras,
+        onehot_offsets.astype(BF16),
+        attended,
+        w_out,
+        projected,
+        probs,
+        normed_low,
+        w_qkv,
     )
-    input_grad = after_grad + input_norm_grad
-
-    def place(part):
-        whole = jnp.zeros((model_width,), F32)
-        return lax.dynamic_update_slice_in_dim(whole, part, column_start, 0)
-
-    gains = lax.psum(jnp.stack([place(gain_attn_mine), place(gain_moe_mine)]), ("dp", "tensor"))
-    router_sum = lax.psum(router_grad.astype(BF16), "dp").astype(F32)
-    qkv_sum = lax.psum(qkv_grad.astype(BF16), "dp").astype(F32)
-    out_proj_sum = lax.psum(out_proj_grad.astype(BF16), "dp").astype(F32)
-    table_sum = lax.psum(table_grad, "dp")
+    loss = jnp.sum(extras[:, experts + 2, 0]) / (2.0 * valid_total * model_width)
+    whole = jnp.swapaxes(extras, 0, 1).reshape(extra_rows, model_width)
+    table_rows = lax.dynamic_index_in_dim(extras, lax.axis_index("tensor"), 0, keepdims=False)
+    table_sum = table_rows[experts + 4 : experts + 4 + heads_here, :BUCKETS].T
+    out_proj_sum = jnp.swapaxes(dense[0].reshape(shards, width_here, width_here), 0, 1)
     return (
         block_out,
         loss,
         input_grad,
-        gains[0],
-        qkv_sum,
-        out_proj_sum,
+        whole[experts],
+        dense[1:].astype(F32),
+        out_proj_sum.reshape(width_here, model_width).astype(F32),
         table_sum,
-        gains[1],
-        router_sum,
+        whole[experts + 1],
+        whole[:experts].T,
         gate_up_grad,
         down_grad,
     )

time: 387 us -> 320 us (0.83)
  blocking collectives: 132 us -> 5.86 us
  Pallas kernels: 117 us -> 213 us
  matrix products: 43.2 us -> 13.6 us
  waiting for transfers between devices: 18.1 us -> 40.6 us
  local copies, waits for them, and re-layouts: 32.6 us -> 11.9 us
  other arithmetic: 16.3 us -> 11.7 us
    psum x6 -> x0, blocking collectives: 126 us -> none  [the longest x1 39.4 us: body(): squared = lax.psum(jnp.sum(deviation * deviation), ('dp', 'tensor'))]
    pallas_call x1 -> x2, Pallas kernels: 7.61 us -> 103 us  [the longest x1 88.7 us: body(): pl.pallas_call(functools.partial(dense_backward, groups, shards, heads_he...]
    dot_general x5 -> x0, matrix products: 20.4 us -> none  [the longest x1 12 us: body(): jnp.einsum('sxmc,jxmf->xjscf', expert_rows, pre_grads, preferred_element_...]
    all_gather x1, waiting for transfers between devices: 7.34 us -> 24.2 us  [body(): w_out_full = lax.all_gather(w_out, 'tensor', axis=0, tiled=True)]
    all_gather x2 -> x1, waiting for transfers between devices: 0.01 us -> 15.9 us  [gather_columns(): return lax.all_gather(values, 'tensor', axis=values.ndim - 1, tiled=True)]
    reshape x3 -> x0, local copies, waits for them, and re-layouts: 15.1 us -> none  [the longest x1 10.6 us: body(): gate_up_grad = gate_up_grad.reshape(w_gate_up.shape)]
    unnamed x42 -> x46, local copies, waits for them, and re-layouts: 16.7 us -> 6.28 us
    psum x1 -> x0, waiting for transfers between devices: 9.97 us -> none  [body(): qkv_sum = lax.psum(qkv_grad.astype(BF16), 'dp').astype(F32)]
  transfers between devices with their start and end apart: 5 -> 2, of which waited for: 2 -> 2; matrix products, arithmetic and copies ran while one was open for 14% -> 1% of each run, Pallas kernels for 0% -> 0%
where the time goes in v3:
time: 320 us; the launch traced here: 315 us
  Pallas kernels  213 us (67%)
  waiting for transfers between devices  40.6 us (13%)
  between operations  18 us (6%)
  matrix products  13.6 us (4%)
  local copies, waits for them, and re-layouts  11.9 us (4%)
  other arithmetic  11.7 us (4%)
  blocking collectives  5.86 us (2%)
    pallas_call x1, Pallas kernels, body(): pl.pallas_call(functools.partial(dense_backward, groups, shards, heads_he...  88.7 us
    pallas_call x1, Pallas kernels, body(): pl.pallas_call(functools.partial(expert_forward, *sizes, chunk), out_shap...  52 us
    pallas_call x1, Pallas kernels, body(): pl.pallas_call(functools.partial(expert_backward, *sizes, chunk), out_sha...  51.5 us
    all_gather x1, waiting for transfers between devices, body(): w_out_full = lax.all_gather(w_out, 'tensor', axis=0, tiled=True)  24.2 us
    all_gather x1, waiting for transfers between devices, gather_columns(): return lax.all_gather(values, 'tensor', axis=values.ndim - 1, tiled=True)  15.9 us
    pallas_call x1, Pallas kernels, body(): pl.pallas_call(functools.partial(weight_grads, shards), grid=(local_exper...  14 us
    dot_general x8, matrix products, dot(): return lax.dot_general(a, b, (dims, ((), ())), preferred_element_type=F32)  7.79 us
    pallas_call x1, Pallas kernels, body(): pl.pallas_call(functools.partial(attention_forward, heads_here, head_widt...  6.59 us
  transfers between devices with their start and end apart: 2, of which 2 were waited for; matrix products, arithmetic and copies ran while one was open for 1% of the time, Pallas kernels for 0%

profile of v3, /device:TPU:0, one launch (start us, length us, event | category | flops | bytes accessed | tf_op | source)
XLA Modules:
  0.0 314.7 jit_solution(13177179690346795468)
XLA Ops:
  7.2 0.0 copy-start
  7.2 0.0 all-gather.3.cloned.1.call-start
  7.2 0.0 copy-start.14
  8.0 1.5 fusion.1
  9.5 1.1 convolution_bitcast_fusion.bias_ref
  10.7 1.5 fusion.3.normed_hbm
  12.2 0.0 copy-start.10
  12.3 0.0 copy-start.19
  12.3 0.0 copy-start.20
  12.3 0.0 copy-start.9
  12.3 1.0 fusion.8.proj_ref.proj_hbm
  13.3 0.0 copy-start.18
  13.3 0.0 copy-start.21
  13.3 6.6 %attention_forward.1 = (bf16[512,256]{1,0:T(8,128)(2,1)}, f32[4,512,512]{2,1,0:T(8,128)S(1)}) custom-call(s32[1]{0:T(128)} %copy.66.len_ref, f32[4,1024]{1,0:T(4,128)S(1)} %convolution_bitcast_fusion.bias_ref, bf16[3,512,256]{2,1,0:T(8,128)(2,1)S(1)} %fusion.8.proj_ref.proj_hbm), custom_call_target="tpu_custom_call" | custom-call | tf_op jit(solution)/shard_map/attention_forward/pallas_call | solution.py:782
  19.9 2.0 copy-done.2
  21.9 0.0 all-gather.3.cloned.1.call-update
  22.0 0.3 all-gather.5.cloned.1.call-start
  22.2 0.5 all-gather.5.cloned.1.call-update
  22.7 0.1 pad.1.clone
  22.8 0.1 pad.3.clone
  22.9 0.1 fusion.32.gains
  23.1 0.2 convert_convert_fusion.onehot
  23.3 2.5 iota_compare_fusion
  25.7 15.9 %all-gather.3.cloned.1.call-done = bf16[512,1024]{1,0:T(8,128)(2,1)} async-done(((bf16[512,256]{1,0:T(8,128)(2,1)}), bf16[512,1024]{1,0:T(8,128)(2,1)}) %all-gather.3.cloned.1.call-update) | async-done | bytes 1048592 | tf_op jit(solution)/shard_map/all_gather | solution.py:771
  41.7 24.2 %all-gather.5.cloned.1.call-done = bf16[1024,1024]{1,0:T(8,128)(2,1)} async-done(((bf16[256,1024]{1,0:T(8,128)(2,1)}), bf16[1024,1024]{1,0:T(8,128)(2,1)}) %all-gather.5.cloned.1.call-update) | async-done | bytes 2097168 | tf_op jit(solution)/shard_map/all_gather | solution.py:794
  65.8 3.3 %multiply_reduce_fusion = (f32[512]{0:T(512)S(1)}, f32[512,1024]{1,0:T(8,128)S(1)}) fusion(bf16[512,1024]{1,0:T(8,128)(2,1)} %all-gather.3.cloned.1.call-done, bf16[1024,1024]{1,0:T(8,128)(2,1)} %all-gather.5.cloned.1.call-done, bf16[512,1024]{1,0:T(8,128)(2,1)S(1)} %copy-done.9), kind=kOutput, calls=%fused_computation.13 | convolution fusion | flops 1075838464 | bytes 6293504 | tf_op jit(solution)/shard_map/dot_general | solution.py:796
  69.1 0.0 copy-start.11
  69.1 0.2 multiply_convert_fusion
  69.4 0.4 fusion.39
  69.9 1.0 copy-done.11
  70.9 0.6 convolution_convert_fusion
  71.5 52.0 %expert_forward.1 = (bf16[8,2,80,256]{3,2,1,0:T(8,128)(2,1)S(1)}, bf16[4,2,640,256]{3,2,1,0:T(8,128)(2,1)}, f32[2,2,640,704]{3,2,1,0:T(8,128)}, bf16[2,640,704]{2,1,0:T(8,128)(2,1)S(1)}, s32[8,128]{1,0:T(8,128)S(1)}) custom-call(bf16[8,2,80,256]{3,2,1,0:T(8,128)(2,1)S(1)} %bitcast.69, bf16[2,2,704,1024]{3,2,1,0:T(8,128)(2,1)} %bitcast.76, ...), custom_call_target="tpu_custom_call" | custom-call | tf_op jit(solution)/shard_map/expert_forward/pallas_call | solution.py:829
  123.6 0.6 fusion.6
  124.2 0.0 copy-start.17
  124.2 0.6 fusion.5
  124.8 0.0 copy-done.7
  124.9 0.5 slice.53
  126.1 1.0 multiply_reduce_fusion.1
  127.1 0.8 copy-done.13
  127.9 0.3 multiply_reduce_fusion.3
  128.2 5.9 %psum.7 = f32[512,2]{0,1:T(2,128)S(1)} all-reduce(f32[512,2]{0,1:T(2,128)S(1)} %pad_maximum_fusion), channel_id=1, replica_groups=mesh['dp'=8,'tensor'=4] {'tensor'}, use_global_device_ids=true, to_apply=%region_8.9 | all-reduce | flops 1024 | bytes 8192 | tf_op jit(solution)/shard_map/psum | solution.py:872
  134.2 0.2 fusion.14
  134.3 1.8 fusion.40
  136.1 0.1 copy.57.scales
  136.3 0.7 pad.2.clone
  137.0 1.0 fusion.4
  138.0 1.0 fusion
  139.0 0.0 copy-start.12
  139.0 51.5 %expert_backward.1 = (bf16[8,2,80,256]{3,2,1,0:T(8,128)(2,1)S(1)}, bf16[4,2,640,256]{3,2,1,0:T(8,128)(2,1)S(1)}, bf16[2,2,640,704]{3,2,1,0:T(8,128)(2,1)}) custom-call(bf16[8,2,80,256]{3,2,1,0:T(8,128)(2,1)S(1)} %bitcast.70, bf16[2,2,704,1024]{3,2,1,0:T(8,128)(2,1)} %bitcast.77, bf16[2,704,1024]{2,1,0:T(8,128)(2,1)} %down_hbm.3, ...), custom_call_target="tpu_custom_call" | custom-call | tf_op jit(solution)/shard_map/expert_backward/pallas_call | solution.py:873
  190.6 0.0 copy-start.6
  190.6 2.1 convolution_add_fusion.1.norm_grad
  192.6 0.1 maximum_maximum_fusion.extras_in
  192.7 88.7 %dense_backward.1 = (bf16[4,1024,256]{2,1,0:T(8,128)(2,1)}, f32[512,256]{1,0:T(8,128)S(1)}, f32[4,24,256]{2,1,0:T(8,128)S(1)}) custom-call(f32[512,256]{1,0:T(8,128)S(1)} %convolution_add_fusion.1.norm_grad, f32[512,256]{1,0:T(8,128)S(1)} %get-tuple-element.47.after, f32[512,256]{1,0:T(8,128)S(1)} %get-tuple-element.48.out_grad, ...), custom_call_target="tpu_custom_call" | custom-call | tf_op jit(solution)/shard_map/dense_backward/pallas_call | solution.py:930
  281.4 0.6 slice_reduce_fusion
  282.0 0.6 fusion.37
  282.6 1.1 slice.57
  283.7 3.3 %slice_convert_fusion = f32[3,1024,256]{2,1,0:T(8,128)} fusion(bf16[4,1024,256]{2,1,0:T(8,128)(2,1)} %get-tuple-element.34), kind=kLoop, calls=%fused_computation.17 | loop fusion | flops 786432 | bytes 4718592 | tf_op jit(solution)/shard_map/convert_element_type | solution.py:1004
  287.1 0.6 slice_bitcast_fusion.7
  287.7 0.6 copy.63
  288.3 0.1 convert_bitcast_fusion
  288.4 1.1 copy.62
  290.2 1.5 copy-done.8
  291.7 14.0 %weight_grads.1 = (f32[2,2,704,1024]{3,2,1,0:T(8,128)}, f32[2,704,1024]{2,1,0:T(8,128)}) custom-call(bf16[4,2,640,256]{3,2,1,0:T(8,128)(2,1)S(1)} %copy-done.4, bf16[4,2,640,256]{3,2,1,0:T(8,128)(2,1)} %copy-done.5, bf16[2,2,640,704]{3,2,1,0:T(8,128)(2,1)} %get-tuple-element.37.side, bf16[2,640,704]{2,1,0:T(8,128)(2,1)S(1)} %copy-done.8), custom_call_target="tpu_custom_call" | custom-call | tf_op jit(solution)/shard_map/weight_grads/pallas_call | solution.py:895
  305.7 0.8 copy.67
  (54 shorter events, 0.4 us)
Async XLA Ops:
  7.2 62.2 %copy-start = (bf16[1024,16]{0,1:T(8,128)(2,1)S(1)}, bf16[1024,16]{0,1:T(8,128)(2,1)}, u32[]{:S(2)}) copy-start(bf16[1024,16]{0,1:T(8,128)(2,1)} %param.23) | copy-start | bytes 98308
  7.2 34.5 %all-gather.3.cloned.1.call-start = ((), (), s32[]{:S(2)}) async-start(), calls=%async_computation | async-start | bytes 1310720 | tf_op jit(solution)/shard_map/all_gather | solution.py:771
  7.2 5.0 %copy-start.14 = (bf16[3,1024,256]{2,1,0:T(8,128)(2,1)S(1)}, bf16[3,1024,256]{2,1,0:T(8,128)(2,1)}, u32[]{:S(2)}) copy-start(bf16[3,1024,256]{2,1,0:T(8,128)(2,1)} %w_qkv_hbm.1) | copy-start | bytes 4718596
  12.2 1.0 copy-start.10
  12.3 10.6 %copy-start.19 = (f32[1024]{0:T(1024)S(1)}, f32[1024]{0:T(1024)}, u32[]{:S(2)}) copy-start(f32[1024]{0:T(1024)} %param.18) | copy-start | bytes 12292
  12.3 10.6 %copy-start.20 = (f32[1024]{0:T(1024)S(1)}, f32[1024]{0:T(1024)}, u32[]{:S(2)}) copy-start(f32[1024]{0:T(1024)} %param.22) | copy-start | bytes 12292
  12.3 10.7 %copy-start.9 = (bf16[512,1024]{1,0:T(8,128)(2,1)S(1)}, bf16[512,1024]{1,0:T(8,128)(2,1)}, u32[]{:S(2)}) copy-start(bf16[512,1024]{1,0:T(8,128)(2,1)} %param.13) | copy-start | bytes 3145732
  13.3 12.4 %copy-start.3 = (bf16[3,512,256]{2,1,0:T(8,128)(2,1)}, bf16[3,512,256]{2,1,0:T(8,128)(2,1)S(1)}, u32[]{:S(2)}) copy-start(bf16[3,512,256]{2,1,0:T(8,128)(2,1)S(1)} %fusion.8.proj_ref.proj_hbm) | copy-start | bytes 2359300
  13.3 9.7 %copy-start.18 = (s32[512,2]{0,1:T(2,128)S(1)}, s32[512,2]{0,1:T(2,128)}, u32[]{:S(2)}) copy-start(s32[512,2]{0,1:T(2,128)} %param.16) | copy-start | bytes 12292
  13.3 9.7 %copy-start.21 = (s32[512,2]{0,1:T(2,128)S(1)}, s32[512,2]{0,1:T(2,128)}, u32[]{:S(2)}) copy-start(s32[512,2]{0,1:T(2,128)} %param.17) | copy-start | bytes 12292
  19.9 2.0 copy-start.2
  22.0 43.9 %all-gather.5.cloned.1.call-start = ((), (), s32[]{:S(2)}) async-start(), calls=%async_computation.1 | async-start | bytes 2621440 | tf_op jit(solution)/shard_map/all_gather | solution.py:794
  69.1 1.7 copy-start.11
  71.5 52.1 %copy-start.15 = (pred[512,2,1280]{2,0,1:T(32,128)(4,1)S(1)}, pred[512,2,1280]{2,0,1:T(32,128)(4,1)}, u32[]{:S(2)}) copy-start(pred[512,2,1280]{2,0,1:T(32,128)(4,1)} %get-tuple-element.53) | copy-start | bytes 3932164
  123.5 1.3 copy-start.7
  124.2 1.9 copy-start.17
  127.1 0.8 copy-start.13
  134.3 2.7 copy-start.16
  139.0 51.5 %copy-start.12 = (bf16[512,2,1280]{2,0,1:T(8,128)(2,1)S(1)}, bf16[512,2,1280]{2,0,1:T(8,128)(2,1)}, u32[]{:S(2)}) copy-start(bf16[512,2,1280]{2,0,1:T(8,128)(2,1)} %get-tuple-element.54) | copy-start | bytes 7864324
  190.5 2.1 copy-start.5
  190.6 2.2 copy-start.6
  287.1 3.1 copy-start.4
  290.2 1.5 copy-start.8
  291.7 14.8 %copy-start.1 = (bf16[1024,16]{0,1:T(8,128)(2,1)S(1)}, bf16[1024,16]{0,1:T(8,128)(2,1)}, u32[]{:S(2)}) copy-start(bf16[1024,16]{0,1:T(8,128)(2,1)} %param.23) | copy-start | bytes 98308
Sparse Core Ops, SparseCore 0:
  22.1 19.5 all-gather.2
  43.2 22.5 all-gather.4
